TPU v7x, 128 devices: a whole 4x4x4 slice. The times are simulated.
128 devices in a mesh: ep: 16 (over x, z), tp: 8 (over y, core).
Axes of the slice: x: 4, y: 4, z: 4, core: 2. Of those that a mesh axis runs over, the one named last changes fastest.
Arguments:
- tokens: bfloat16 [2048, 4096], P('ep', 'tp'), may hold values from -6 to 6
- out_grad: bfloat16 [2048, 4096], P('ep', 'tp'), may hold values from -6 to 6
- routes: int32 [2048, 4], P('ep'), may hold values from 0 to 15, all different within a row; in each aligned block of 128 rows (0 to 127, 128 to 255, ...) at most 64 rows name the same one
- probs: bfloat16 [2048, 4], P('ep'), may hold values from 0.019897461 to 0.59765625
- w_in: bfloat16 [16, 2, 1536, 4096], P('ep', None, 'tp'), as said below
- w_out: bfloat16 [16, 1536, 4096], P('ep', 'tp'), as said below
Outputs:
- in_grad: bfloat16 [2048, 4096], P('ep', 'tp')
- grad_in: bfloat16 [16, 2, 1536, 4096], P('ep', None, 'tp')
- grad_out: bfloat16 [16, 1536, 4096], P('ep', 'tp')
Inputs may be any that keep to these rules, and one draw needn't show every extreme that they name: `routes`: each token names 4 different copies; within the tokens of one device (aligned blocks of 128 tokens) no copy is named more than 64 times, a bound that some block reaches. `w_in`: copies c and c + 8 hold equal weights. `w_out`: copies c and c + 8 hold equal weights.
All inputs are finite; a program needn't handle non-finite values.
Results may differ from a plain program's by a relative error of at most 0.02.
Values may be sent and summed in bfloat16 or wider, within the bound.
A program may use at most 128 MiB of HBM per device.

v0:
```python
import jax
import jax.numpy as jnp
from jax import lax
from jax.sharding import PartitionSpec as P


def partner(block, axis, apart):
    count = lax.axis_size(axis)
    route = []
    for low in range(count):
        high = low | 1 << apart
        if high != low and high < count:
            route += [(low, high), (high, low)]
    return lax.ppermute(block, axis, route)


def slot_tables(block_routes, copies, cap):
    flat = block_routes.reshape(-1)
    nrows = flat.shape[0]
    onehot = (flat[:, None] == jnp.arange(copies, dtype=jnp.int32)[None, :]).astype(jnp.int32)
    ranks = jnp.sum((jnp.cumsum(onehot, axis=0) - 1) * onehot, axis=1)
    slot = flat * cap + ranks
    source = (
        jnp.full((copies * cap,), nrows, jnp.int32).at[slot].set(jnp.arange(nrows, dtype=jnp.int32))
    )
    return (slot, source)


def body(tokens, out_grad, routes, probs, w_in, w_out):
    n_ep = lax.axis_size("ep")
    tok_dev, top = routes.shape
    nrows = tok_dev * top
    cap = 2 * nrows // n_ep
    slot, source = slot_tables(routes, n_ep, cap)
    valid = source < nrows
    local = jnp.minimum(source, nrows - 1)
    tok_index = local // top
    scale = jnp.where(valid, probs.reshape(-1)[local].astype(jnp.float32), 0.0)[:, None]
    full_x, full_g = (
        lax.all_gather(tokens, "tp", axis=1, tiled=True),
        lax.all_gather(out_grad, "tp", axis=1, tiled=True),
    )
    packed_x = jnp.where(valid[:, None], full_x[tok_index], jnp.zeros((), jnp.bfloat16))
    packed_g = (scale * full_g[tok_index].astype(jnp.float32)).astype(jnp.bfloat16)
    width = full_x.shape[1]
    send_x = packed_x.reshape(n_ep, cap, width)
    send_g = packed_g.reshape(n_ep, cap, width)
    recv_x, recv_g = (
        lax.all_to_all(send_x, "ep", split_axis=0, concat_axis=0, tiled=True),
        lax.all_to_all(send_g, "ep", split_axis=0, concat_axis=0, tiled=True),
    )
    width = recv_x.shape[2]
    rows_x = recv_x.reshape(n_ep * cap, width)
    rows_g = recv_g.reshape(n_ep * cap, width)
    w_gate = w_in[0, 0]
    w_up = w_in[0, 1]
    w_down = w_out[0]
    contract_last = (((1,), (1,)), ((), ()))
    a = lax.dot_general(rows_x, w_gate, contract_last, preferred_element_type=jnp.float32)
    b = lax.dot_general(rows_x, w_up, contract_last, preferred_element_type=jnp.float32)
    sig = jax.nn.sigmoid(a)
    silu = a * sig
    hidden = (silu * b).astype(jnp.bfloat16)
    dh = lax.dot_general(rows_g, w_down, contract_last, preferred_element_type=jnp.float32)
    da = (dh * b * sig * (1.0 + a * (1.0 - sig))).astype(jnp.bfloat16)
    db = (dh * silu).astype(jnp.bfloat16)
    partial_rows = jnp.dot(da, w_gate, preferred_element_type=jnp.float32)
    partial_rows = partial_rows + jnp.dot(db, w_up, preferred_element_type=jnp.float32)
    summed = lax.psum_scatter(
        partial_rows.reshape(n_ep, cap, width).astype(jnp.bfloat16),
        "tp",
        scatter_dimension=2,
        tiled=True,
    )
    back = lax.all_to_all(summed, "ep", split_axis=0, concat_axis=0, tiled=True)
    picked = back.reshape(n_ep * cap, back.shape[2])[slot]
    in_grad = jnp.sum(
        picked.astype(jnp.float32).reshape(tok_dev, top, back.shape[2]), axis=1
    ).astype(jnp.bfloat16)
    contract_rows = (((0,), (0,)), ((), ()))
    own_in = jnp.stack(
        [
            lax.dot_general(da, rows_x, contract_rows, preferred_element_type=jnp.float32),
            lax.dot_general(db, rows_x, contract_rows, preferred_element_type=jnp.float32),
        ]
    ).astype(jnp.bfloat16)[None]
    own_out = lax.dot_general(
        hidden, rows_g, contract_rows, preferred_element_type=jnp.float32
    ).astype(jnp.bfloat16)[None]
    half_bit = n_ep.bit_length() - 2
    other_in, other_out = partner((own_in, own_out), "ep", half_bit)
    grad_in = (own_in.astype(jnp.float32) + other_in.astype(jnp.float32)).astype(jnp.bfloat16)
    grad_out = (own_out.astype(jnp.float32) + other_out.astype(jnp.float32)).astype(jnp.bfloat16)
    return (in_grad, grad_in, grad_out)


def solution(mesh):
    return jax.shard_map(
        body,
        mesh=mesh,
        in_specs=(
            P("ep", "tp"),
            P("ep", "tp"),
            P("ep", None),
            P("ep", None),
            P("ep", None, "tp", None),
            P("ep", "tp", None),
        ),
        out_specs=(P("ep", "tp"), P("ep", None, "tp", None), P("ep", "tp", None)),
        check_vma=False,
    )
```

profile of v0, /device:TPU:0, one launch (start us, length us, event | category | flops | bytes accessed | tf_op | source)
XLA Modules:
  0.0 534.7 jit_solution(16174911186118901653)
XLA Ops:
  7.9 0.8 copy.10
  8.9 1.2 reduce-window.6
  11.3 0.8 copy.13
  12.3 2.4 scatter_custom_fusion
  14.8 6.8 %gather_fusion = bf16[1024]{0:T(1024)(128)(2,1)S(1)} fusion(bf16[512]{0:T(512)(128)(2,1)S(1)} %reshape.144, s32[1024]{0:T(1024)S(1)} %get-tuple-element.7), kind=kCustom, calls=%fused_computation | custom fusion | bytes 8192 | tf_op jit(solution)/shard_map/gather | solution.py:38
  21.7 13.9 %all-gather.5.cloned.1.call-done = bf16[128,4096]{1,0:T(8,128)(2,1)} async-done(((bf16[128,512]{1,0:T(8,128)(2,1)}), bf16[128,4096]{1,0:T(8,128)(2,1)}) %all-gather.5.cloned.1.call-update) | async-done | bytes 1048592 | tf_op jit(solution)/shard_map/all_gather | solution.py:40
  35.6 16.4 %gather_fusion.2 = bf16[1024,4096]{1,0:T(8,128)(2,1)} fusion(bf16[128,4096]{1,0:T(8,128)(2,1)} %all-gather.5.cloned.1.call-done, s32[1024]{0:T(1024)S(1)} %get-tuple-element.8), kind=kCustom, calls=%fused_computation.2 | custom fusion | bytes 16781312 | tf_op jit(solution)/shard_map/gather | solution.py:43
  52.0 7.2 %broadcast_select_fusion = bf16[16,64,4096]{2,1,0:T(8,128)(2,1)} fusion(bf16[16,64,4096]{2,1,0:T(8,128)(2,1)} %bitcast.56, pred[16,64]{1,0:T(8,128)(4,1)S(1)} %broadcast_in_dim.35), kind=kLoop, calls=%fused_computation.8 | loop fusion | flops 4194304 | bytes 16778240 | tf_op jit(solution)/shard_map/jit(_where)/select_n | solution.py:43
  59.2 7.0 %all-to-all-start.1 = ((bf16[16,64,4096]{2,1,0:T(8,128)(2,1)}), bf16[16,64,4096]{2,1,0:T(8,128)(2,1)}, u32[]{:S(2)}, u32[]{:S(2)}) async-start(bf16[16,64,4096]{2,1,0:T(8,128)(2,1)} %broadcast_select_fusion), calls=%async_computation.1 | async-start | bytes 16777216 | tf_op jit(solution)/shard_map/all_to_all | solution.py:49
  67.1 25.2 %all-gather.3.cloned.1.call-done = bf16[128,4096]{1,0:T(8,128)(2,1)} async-done(((bf16[128,512]{1,0:T(8,128)(2,1)}), bf16[128,4096]{1,0:T(8,128)(2,1)}) %all-gather.3.cloned.1.call-update) | async-done | bytes 1048592 | tf_op jit(solution)/shard_map/all_gather | solution.py:41
  92.3 16.4 %gather_fusion.1 = bf16[1024,4096]{1,0:T(8,128)(2,1)} fusion(bf16[128,4096]{1,0:T(8,128)(2,1)} %all-gather.3.cloned.1.call-done, s32[1024]{0:T(1024)S(1)} %get-tuple-element.8), kind=kCustom, calls=%fused_computation.1 | custom fusion | bytes 16781312 | tf_op jit(solution)/shard_map/gather | solution.py:44
  108.7 10.0 %fusion = bf16[16,64,4096]{2,1,0:T(8,128)(2,1)} fusion(bf16[16,64,4096]{2,1,0:T(8,128)(2,1)} %bitcast.57, f32[16,64]{1,0:T(8,128)S(1)} %mul.55), kind=kLoop, calls=%fused_computation.6 | loop fusion | flops 12582912 | bytes 16781312 | tf_op jit(solution)/shard_map/convert_element_type | solution.py:44
  118.7 93.8 %all-to-all-done.1 = bf16[16,64,4096]{2,1,0:T(8,128)(2,1)} async-done(((bf16[16,64,4096]{2,1,0:T(8,128)(2,1)}), bf16[16,64,4096]{2,1,0:T(8,128)(2,1)}, u32[]{:S(2)}, u32[]{:S(2)}) %all-to-all-start.1) | async-done | bytes 8388640 | tf_op jit(solution)/shard_map/all_to_all | solution.py:49
  212.5 11.8 %all-to-all-start = ((bf16[16,64,4096]{2,1,0:T(8,128)(2,1)}), bf16[16,64,4096]{2,1,0:T(8,128)(2,1)}, u32[]{:S(2)}, u32[]{:S(2)}) async-start(bf16[16,64,4096]{2,1,0:T(8,128)(2,1)} %fusion), calls=%async_computation | async-start | bytes 16777216 | tf_op jit(solution)/shard_map/all_to_all | solution.py:50
  224.5 6.8 %fusion.6 = f32[1024,192]{0,1:T(8,128)S(1)} fusion(bf16[1024,4096]{1,0:T(8,128)(2,1)} %bitcast.7, bf16[1,2,192,4096]{3,2,1,0:T(8,128)(2,1)} %param.10), kind=kOutput, calls=%fused_computation.20 | convolution fusion | flops 1610612736 | bytes 10747904 | tf_op jit(solution)/shard_map/dot_general | solution.py:59
  231.4 7.2 %fusion.9 = f32[1024,192]{0,1:T(8,128)} fusion(bf16[1024,4096]{1,0:T(8,128)(2,1)} %bitcast.7, bf16[1,2,192,4096]{3,2,1,0:T(8,128)(2,1)S(1)} %copy-done.3), kind=kOutput, calls=%fused_computation.23 | convolution fusion | flops 1610612736 | bytes 10747904 | tf_op jit(solution)/shard_map/dot_general | solution.py:60
  238.5 119.4 %all-to-all-done = bf16[16,64,4096]{2,1,0:T(8,128)(2,1)} async-done(((bf16[16,64,4096]{2,1,0:T(8,128)(2,1)}), bf16[16,64,4096]{2,1,0:T(8,128)(2,1)}, u32[]{:S(2)}, u32[]{:S(2)}) %all-to-all-start) | async-done | bytes 8388640 | tf_op jit(solution)/shard_map/all_to_all | solution.py:50
  357.9 6.7 %multiply_convert_fusion.1 = (bf16[1024,192]{0,1:T(8,128)(2,1)S(1)}, bf16[1024,192]{0,1:T(8,128)(2,1)S(1)}) fusion(f32[1024,192]{0,1:T(8,128)S(1)} %fusion.6, f32[1024,192]{0,1:T(8,128)} %fusion.9, bf16[1024,4096]{1,0:T(8,128)(2,1)} %bitcast.4, bf16[1,192,4096]{2,1,0:T(8,128)(2,1)S(1)} %copy-done), kind=kOutput, calls=%fused_computation.32 | convolution fusion | flops 1613168640 | bytes 12320768 | tf_op jit(solution)/shard_map/dot_general | solution.py:64
  364.6 8.1 %fusion.4 = f32[1024,4096]{1,0:T(8,128)} fusion(bf16[1024,192]{0,1:T(8,128)(2,1)S(1)} %get-tuple-element.6, bf16[1,2,192,4096]{3,2,1,0:T(8,128)(2,1)S(1)} %copy-done.4), kind=kOutput, calls=%fused_computation.18 | convolution fusion | flops 1610612736 | bytes 18743296 | tf_op jit(solution)/shard_map/dot_general | solution.py:67
  372.8 11.4 %add_convert_fusion = bf16[1024,4096]{1,0:T(8,128)(2,1)} fusion(f32[1024,4096]{1,0:T(8,128)} %fusion.4, bf16[1024,192]{0,1:T(8,128)(2,1)S(1)} %get-tuple-element.5, bf16[1,2,192,4096]{3,2,1,0:T(8,128)(2,1)S(1)} %copy-done.4), kind=kOutput, calls=%fused_computation.7 | convolution fusion | flops 1619001344 | bytes 27131904 | tf_op jit(solution)/shard_map/dot_general | solution.py:68
  384.2 5.4 %fusion.1 = bf16[1,1,192,4096]{3,2,1,0:T(8,128)(2,1)S(1)} fusion(bf16[1024,192]{0,1:T(8,128)(2,1)S(1)} %get-tuple-element.6, bf16[1024,4096]{1,0:T(8,128)(2,1)} %bitcast.7), kind=kOutput, calls=%fused_computation.13 | convolution fusion | flops 1611399168 | bytes 10354688 | tf_op jit(solution)/shard_map/dot_general | solution.py:83
  389.7 5.8 %fusion.2 = bf16[1,1,192,4096]{3,2,1,0:T(8,128)(2,1)S(1)} fusion(bf16[1024,192]{0,1:T(8,128)(2,1)S(1)} %get-tuple-element.5, bf16[1024,4096]{1,0:T(8,128)(2,1)} %bitcast.7), kind=kOutput, calls=%fused_computation.14 | convolution fusion | flops 1611399168 | bytes 10354688 | tf_op jit(solution)/shard_map/dot_general | solution.py:84
  395.4 1.9 pad_maximum_fusion
  397.6 5.3 fusion.3
  402.9 3.7 collective-permute-start.1
  406.6 92.6 %collective-permute-done.1 = bf16[1,192,4096]{2,1,0:T(8,128)(2,1)S(1)} collective-permute-done((bf16[1,192,4096]{2,1,0:T(8,128)(2,1)S(1)}, bf16[1,192,4096]{2,1,0:T(8,128)(2,1)S(1)}, u32[]{:S(2)}, u32[]{:S(2)}) %collective-permute-start.1) | collective-permute-done | bytes 1572896 | tf_op jit(solution)/shard_map/ppermute | solution.py:14
  499.2 1.7 add_convert_fusion.2
  500.9 9.9 %all-to-all-start.2 = ((bf16[16,64,512]{2,1,0:T(8,128)(2,1)}), bf16[16,64,512]{2,1,0:T(8,128)(2,1)S(1)}, u32[]{:S(2)}, u32[]{:S(2)}) async-start(bf16[16,64,512]{2,1,0:T(8,128)(2,1)} %reduce-scatter.2.cloned.1.call-done), calls=%async_computation.3 | async-start | bytes 2097152 | tf_op jit(solution)/shard_map/all_to_all | solution.py:75
  510.8 5.8 %add_convert_fusion.1 = bf16[1,2,192,4096]{3,2,1,0:T(8,128)(2,1)} fusion(bf16[1,2,192,4096]{3,2,1,0:T(8,128)(2,1)} %collective-permute-done, bf16[1,1,192,4096]{3,2,1,0:T(8,128)(2,1)} %copy-done.2, bf16[1,1,192,4096]{3,2,1,0:T(8,128)(2,1)} %copy-done.1), kind=kLoop, calls=%fused_computation.9 | loop fusion | flops 7864320 | bytes 9437184 | tf_op jit(solution)/shard_map/convert_element_type | solution.py:92
  516.6 8.2 %all-to-all-done.2 = bf16[16,64,512]{2,1,0:T(8,128)(2,1)S(1)} async-done(((bf16[16,64,512]{2,1,0:T(8,128)(2,1)}), bf16[16,64,512]{2,1,0:T(8,128)(2,1)S(1)}, u32[]{:S(2)}, u32[]{:S(2)}) %all-to-all-start.2) | async-done | bytes 1048608 | tf_op jit(solution)/shard_map/all_to_all | solution.py:75
  524.7 2.0 gather_fusion.3
  526.8 1.3 reduce_sum.25
  (40 shorter events, 3.9 us)
Async XLA Ops:
  7.2 350.7 %copy-start = (bf16[1,192,4096]{2,1,0:T(8,128)(2,1)S(1)}, bf16[1,192,4096]{2,1,0:T(8,128)(2,1)}, u32[]{:S(2)}) copy-start(bf16[1,192,4096]{2,1,0:T(8,128)(2,1)} %param.11) | copy-start | bytes 4718596
  7.2 28.4 %all-gather.5.cloned.1.call-start = ((), (), s32[]{:S(2)}) async-start(), calls=%async_computation.5 | async-start | bytes 1179648 | tf_op jit(solution)/shard_map/all_gather | solution.py:40
  59.2 153.3 %all-to-all-start.1 = ((bf16[16,64,4096]{2,1,0:T(8,128)(2,1)}), bf16[16,64,4096]{2,1,0:T(8,128)(2,1)}, u32[]{:S(2)}, u32[]{:S(2)}) async-start(bf16[16,64,4096]{2,1,0:T(8,128)(2,1)} %broadcast_select_fusion), calls=%async_computation.1 | async-start | bytes 16777216 | tf_op jit(solution)/shard_map/all_to_all | solution.py:49
  66.3 26.0 %all-gather.3.cloned.1.call-start = ((), (), s32[]{:S(2)}) async-start(), calls=%async_computation.4 | async-start | bytes 1179648 | tf_op jit(solution)/shard_map/all_gather | solution.py:41
  212.5 145.4 %all-to-all-start = ((bf16[16,64,4096]{2,1,0:T(8,128)(2,1)}), bf16[16,64,4096]{2,1,0:T(8,128)(2,1)}, u32[]{:S(2)}, u32[]{:S(2)}) async-start(bf16[16,64,4096]{2,1,0:T(8,128)(2,1)} %fusion), calls=%async_computation | async-start | bytes 16777216 | tf_op jit(solution)/shard_map/all_to_all | solution.py:50
  224.3 276.6 %reduce-scatter.2.cloned.1.call-start = ((), (), s32[]{:S(2)}) async-start(), calls=%async_computation.6 | async-start | bytes 9437184 | tf_op jit(solution)/shard_map/reduce_scatter | solution.py:69
  224.5 6.9 %copy-start.3 = (bf16[1,2,192,4096]{3,2,1,0:T(8,128)(2,1)S(1)}, bf16[1,2,192,4096]{3,2,1,0:T(8,128)(2,1)}, u32[]{:S(2)}) copy-start(bf16[1,2,192,4096]{3,2,1,0:T(8,128)(2,1)} %param.10) | copy-start | bytes 9437188
  357.9 6.7 %copy-start.4 = (bf16[1,2,192,4096]{3,2,1,0:T(8,128)(2,1)S(1)}, bf16[1,2,192,4096]{3,2,1,0:T(8,128)(2,1)}, u32[]{:S(2)}) copy-start(bf16[1,2,192,4096]{3,2,1,0:T(8,128)(2,1)} %param.10) | copy-start | bytes 9437188
  389.6 5.8 %copy-start.1 = (bf16[1,1,192,4096]{3,2,1,0:T(8,128)(2,1)}, bf16[1,1,192,4096]{3,2,1,0:T(8,128)(2,1)S(1)}, u32[]{:S(2)}) copy-start(bf16[1,1,192,4096]{3,2,1,0:T(8,128)(2,1)S(1)} %fusion.1) | copy-start | bytes 4718596
  395.4 2.2 copy-start.2
  395.4 2.2 copy-start.5
  397.6 113.2 %collective-permute-start = (bf16[1,2,192,4096]{3,2,1,0:T(8,128)(2,1)}, bf16[1,2,192,4096]{3,2,1,0:T(8,128)(2,1)}, u32[]{:S(2)}, u32[]{:S(2)}) collective-permute-start(bf16[1,2,192,4096]{3,2,1,0:T(8,128)(2,1)} %pad_maximum_fusion), channel_id=1, source_target_pairs={{0,64},{64,0},{8,72},{72,8},{16,80},{80,16},{24,88},{88,24},{32,96... | collective-permute-start | bytes 9437192 | tf_op jit(solution)/shard_map/ppermute | solution.py:14
  402.9 96.3 %collective-permute-start.1 = (bf16[1,192,4096]{2,1,0:T(8,128)(2,1)S(1)}, bf16[1,192,4096]{2,1,0:T(8,128)(2,1)S(1)}, u32[]{:S(2)}, u32[]{:S(2)}) collective-permute-start(bf16[1,192,4096]{2,1,0:T(8,128)(2,1)S(1)} %fusion.3), channel_id=1, source_target_pairs={{0,64},{64,0},{8,72},{72,8},{16,80},{80,16},{24,88},{88,24},{32,96... | collective-permute-start | bytes 4718600 | tf_op jit(solution)/shard_map/ppermute | solution.py:14
  500.9 23.9 %all-to-all-start.2 = ((bf16[16,64,512]{2,1,0:T(8,128)(2,1)}), bf16[16,64,512]{2,1,0:T(8,128)(2,1)S(1)}, u32[]{:S(2)}, u32[]{:S(2)}) async-start(bf16[16,64,512]{2,1,0:T(8,128)(2,1)} %reduce-scatter.2.cloned.1.call-done), calls=%async_computation.3 | async-start | bytes 2097152 | tf_op jit(solution)/shard_map/all_to_all | solution.py:75
Sparse Core Ops, SparseCore 0:
  9.7 25.8 all-gather.4
  68.8 23.4 all-gather.2
  384.3 54.3 reduce-scatter.1
where the time goes:
time: 535 us
  waiting for transfers between devices  354 us (66%)
  matrix products  56.7 us (11%)
  local copies, waits for them, and re-layouts  47 us (9%)
  starting transfers between devices  32.6 us (6%)
  other arithmetic  30 us (6%)
  between operations  14 us (3%)
    all_to_all x1, waiting for transfers between devices, body(): lax.all_to_all(send_g, 'ep', split_axis=0, concat_axis=0, tiled=True)  119 us
    all_to_all x1, waiting for transfers between devices, body(): lax.all_to_all(send_x, 'ep', split_axis=0, concat_axis=0, tiled=True)  93.8 us
    ppermute x2, waiting for transfers between devices, partner(): return lax.ppermute(block, axis, route)  92.6 us
    all_gather x1, waiting for transfers between devices, body(): lax.all_gather(out_grad, 'tp', axis=1, tiled=True)  25.2 us
    gather x1, local copies, waits for them, and re-layouts, body(): full_g[tok_index].astype(jnp.float32)  16.4 us
    gather x1, local copies, waits for them, and re-layouts, body(): full_x[tok_index]  16.4 us
    all_gather x1, waiting for transfers between devices, body(): lax.all_gather(tokens, 'tp', axis=1, tiled=True)  13.9 us
    all_to_all x1, starting transfers between devices, body(): lax.all_to_all(send_g, 'ep', split_axis=0, concat_axis=0, tiled=True)  11.8 us
  transfers between devices with their start and end apart: 8, of which 6 were waited for; matrix products, arithmetic and copies ran while one was open for 15% of the time, Pallas kernels for 0%

commit v1 on v0

--- a/solution.py
+++ b/solution.py
@@ -17,8 +17,9 @@
 def slot_tables(block_routes, copies, cap):
     flat = block_routes.reshape(-1)
     nrows = flat.shape[0]
-    onehot = (flat[:, None] == jnp.arange(copies, dtype=jnp.int32)[None, :]).astype(jnp.int32)
-    ranks = jnp.sum((jnp.cumsum(onehot, axis=0) - 1) * onehot, axis=1)
+    before = jnp.arange(nrows, dtype=jnp.int32)
+    earlier = (before[None, :] < before[:, None]) & (flat[None, :] == flat[:, None])
+    ranks = jnp.sum(earlier.astype(jnp.int32), axis=1)
     slot = flat * cap + ranks
     source = (
         jnp.full((copies * cap,), nrows, jnp.int32).at[slot].set(jnp.arange(nrows, dtype=jnp.int32))
@@ -36,22 +37,18 @@
     local = jnp.minimum(source, nrows - 1)
     tok_index = local // top
     scale = jnp.where(valid, probs.reshape(-1)[local].astype(jnp.float32), 0.0)[:, None]
-    full_x, full_g = (
-        lax.all_gather(tokens, "tp", axis=1, tiled=True),
-        lax.all_gather(out_grad, "tp", axis=1, tiled=True),
-    )
-    packed_x = jnp.where(valid[:, None], full_x[tok_index], jnp.zeros((), jnp.bfloat16))
-    packed_g = (scale * full_g[tok_index].astype(jnp.float32)).astype(jnp.bfloat16)
-    width = full_x.shape[1]
-    send_x = packed_x.reshape(n_ep, cap, width)
-    send_g = packed_g.reshape(n_ep, cap, width)
+    packed_x = jnp.where(valid[:, None], tokens[tok_index], jnp.zeros((), jnp.bfloat16))
+    packed_g = (scale * out_grad[tok_index].astype(jnp.float32)).astype(jnp.bfloat16)
+    part = tokens.shape[1]
+    send_x = packed_x.reshape(n_ep, cap, part)
+    send_g = packed_g.reshape(n_ep, cap, part)
     recv_x, recv_g = (
         lax.all_to_all(send_x, "ep", split_axis=0, concat_axis=0, tiled=True),
         lax.all_to_all(send_g, "ep", split_axis=0, concat_axis=0, tiled=True),
     )
-    width = recv_x.shape[2]
-    rows_x = recv_x.reshape(n_ep * cap, width)
-    rows_g = recv_g.reshape(n_ep * cap, width)
+    rows_x = lax.all_gather(recv_x.reshape(n_ep * cap, part), "tp", axis=1, tiled=True)
+    rows_g = lax.all_gather(recv_g.reshape(n_ep * cap, part), "tp", axis=1, tiled=True)
+    width = rows_x.shape[1]
     w_gate = w_in[0, 0]
     w_up = w_in[0, 1]
     w_down = w_out[0]

time: 535 us -> 330 us (0.62)
  waiting for transfers between devices: 354 us -> 176 us
  blocking collectives: 0 us -> 44.4 us
  local copies, waits for them, and re-layouts: 47 us -> 21.8 us
  starting transfers between devices: 32.6 us -> 10.7 us
  other arithmetic: 30 us -> 11.9 us
  matrix products: 56.7 us -> 50.8 us
    all_to_all x2 -> x0, waiting for transfers between devices: 213 us -> none  [the longest x1 119 us: body(): lax.all_to_all(send_g, 'ep', split_axis=0, concat_axis=0, tiled=True)]
    all_to_all x0 -> x2, blocking collectives: none -> 44.4 us  [the longest x1 24.7 us: body(): lax.all_to_all(send_x, 'ep', split_axis=0, concat_axis=0, tiled=True)]
    gather x2, local copies, waits for them, and re-layouts: 32.9 us -> 7.92 us  [the longest x1 3.96 us: body(): tokens[tok_index]]
    all_gather x2, waiting for transfers between devices: 39.1 us -> 64 us  [the longest x1 40.1 us: body(): lax.all_gather(recv_g.reshape(n_ep * cap, part), 'tp', axis=1, tiled=True)]
    all_to_all x2 -> x0, starting transfers between devices: 18.7 us -> none  [the longest x1 11.8 us: body(): lax.all_to_all(send_g, 'ep', split_axis=0, concat_axis=0, tiled=True)]
    convert_element_type x2 -> x1, other arithmetic: 9.98 us -> 0.3 us  [body(): (scale * out_grad[tok_index].astype(jnp.float32)).astype(jnp.bfloat16)]
    ppermute x2, waiting for transfers between devices: 92.6 us -> 100 us  [partner(): return lax.ppermute(block, axis, route)]
    select_n x1, other arithmetic: 7.23 us -> 0.2 us  [body(): jnp.where(valid[:, None], tokens[tok_index], jnp.zeros((), jnp.bfloat16))]
  transfers between devices with their start and end apart: 8 -> 6, of which waited for: 6 -> 4; matrix products, arithmetic and copies ran while one was open for 15% -> 11% of each run, Pallas kernels for 0% -> 0%
where the time goes in v1:
time: 330 us
  waiting for transfers between devices  176 us (53%)
  matrix products  50.8 us (15%)
  blocking collectives  44.4 us (13%)
  local copies, waits for them, and re-layouts  21.8 us (7%)
  between operations  14 us (4%)
  other arithmetic  11.9 us (4%)
  starting transfers between devices  10.7 us (3%)
    ppermute x2, waiting for transfers between devices, partner(): return lax.ppermute(block, axis, route)  100 us
    all_gather x1, waiting for transfers between devices, body(): lax.all_gather(recv_g.reshape(n_ep * cap, part), 'tp', axis=1, tiled=True)  40.1 us
    all_to_all x1, blocking collectives, body(): lax.all_to_all(send_x, 'ep', split_axis=0, concat_axis=0, tiled=True)  24.7 us
    all_gather x1, waiting for transfers between devices, body(): lax.all_gather(recv_x.reshape(n_ep * cap, part), 'tp', axis=1, tiled=True)  23.9 us
    all_to_all x1, blocking collectives, body(): lax.all_to_all(send_g, 'ep', split_axis=0, concat_axis=0, tiled=True)  19.7 us
    all_to_all x1, waiting for transfers between devices, body(): back = lax.all_to_all(summed, 'ep', split_axis=0, concat_axis=0, tiled=True)  11.8 us
    dot_general x1, matrix products, body(): jnp.dot(db, w_up, preferred_element_type=jnp.float32)  11.4 us
    dot_general x1, matrix products, body(): partial_rows = jnp.dot(da, w_gate, preferred_element_type=jnp.float32)  8.15 us
  transfers between devices with their start and end apart: 6, of which 4 were waited for; matrix products, arithmetic and copies ran while one was open for 11% of the time, Pallas kernels for 0%

profile of v1, /device:TPU:0, one launch (start us, length us, event | category | flops | bytes accessed | tf_op | source)
XLA Modules:
  0.0 329.8 jit_solution(15195773333764695855)
XLA Ops:
  7.2 0.8 broadcast_multiply_fusion
  8.0 0.8 copy.13
  8.8 0.8 copy.14
  10.1 0.3 convert_reduce_fusion
  10.4 2.4 scatter_custom_fusion
  12.9 6.8 %gather_fusion = bf16[1024]{0:T(1024)(128)(2,1)S(1)} fusion(bf16[512]{0:T(512)(128)(2,1)S(1)} %reshape.126, s32[1024]{0:T(1024)S(1)} %get-tuple-element.7), kind=kCustom, calls=%fused_computation | custom fusion | bytes 8192 | tf_op jit(solution)/shard_map/gather | solution.py:39
  19.8 4.0 %gather_fusion.2 = bf16[1024,512]{1,0:T(8,128)(2,1)S(1)} fusion(bf16[128,512]{1,0:T(8,128)(2,1)S(1)} %copy-done.2, s32[1024]{0:T(1024)S(1)} %get-tuple-element.8), kind=kCustom, calls=%fused_computation.2 | custom fusion | bytes 2101248 | tf_op jit(solution)/shard_map/gather | solution.py:40
  24.0 24.7 %all_to_all.15 = bf16[16,64,512]{2,1,0:T(8,128)(2,1)} all-to-all(bf16[16,64,512]{2,1,0:T(8,128)(2,1)S(1)} %broadcast_select_fusion), channel_id=1, replica_groups=mesh['ep'=16,'tp'=8] {'ep'}, dimensions={0} | all-to-all | bytes 2097152 | tf_op jit(solution)/shard_map/all_to_all | solution.py:46
  48.8 4.0 %gather_fusion.1 = bf16[1024,512]{1,0:T(8,128)(2,1)S(1)} fusion(bf16[128,512]{1,0:T(8,128)(2,1)S(1)} %copy-done.3, s32[1024]{0:T(1024)S(1)} %get-tuple-element.8), kind=kCustom, calls=%fused_computation.1 | custom fusion | bytes 2101248 | tf_op jit(solution)/shard_map/gather | solution.py:41
  52.8 0.3 fusion.3
  53.1 19.7 %all_to_all.16 = bf16[16,64,512]{2,1,0:T(8,128)(2,1)} all-to-all(bf16[16,64,512]{2,1,0:T(8,128)(2,1)S(1)} %fusion.3), channel_id=1, replica_groups=mesh['ep'=16,'tp'=8] {'ep'}, dimensions={0} | all-to-all | bytes 2097152 | tf_op jit(solution)/shard_map/all_to_all | solution.py:47
  73.0 23.9 %all-gather.5.cloned.1.call-done = bf16[1024,4096]{1,0:T(8,128)(2,1)} async-done(((bf16[1024,512]{1,0:T(8,128)(2,1)}), bf16[1024,4096]{1,0:T(8,128)(2,1)}) %all-gather.5.cloned.1.call-update) | async-done | bytes 8388624 | tf_op jit(solution)/shard_map/all_gather | solution.py:49
  96.9 7.7 %fusion.6 = f32[1024,192]{0,1:T(8,128)} fusion(bf16[1024,4096]{1,0:T(8,128)(2,1)} %all-gather.5.cloned.1.call-done, bf16[1,2,192,4096]{3,2,1,0:T(8,128)(2,1)} %param.10), kind=kOutput, calls=%fused_computation.19 | convolution fusion | flops 1610612736 | bytes 10747904 | tf_op jit(solution)/shard_map/dot_general | solution.py:56
  104.6 3.8 %fusion.9 = f32[1024,192]{0,1:T(8,128)} fusion(bf16[1024,4096]{1,0:T(8,128)(2,1)S(1)} %copy-done.7, bf16[1,2,192,4096]{3,2,1,0:T(8,128)(2,1)S(1)} %copy-done.5), kind=kOutput, calls=%fused_computation.22 | convolution fusion | flops 1610612736 | bytes 10747904 | tf_op jit(solution)/shard_map/dot_general | solution.py:57
  108.4 40.1 %all-gather.3.cloned.1.call-done = bf16[1024,4096]{1,0:T(8,128)(2,1)} async-done(((bf16[1024,512]{1,0:T(8,128)(2,1)}), bf16[1024,4096]{1,0:T(8,128)(2,1)}) %all-gather.3.cloned.1.call-update) | async-done | bytes 8388624 | tf_op jit(solution)/shard_map/all_gather | solution.py:50
  148.5 6.9 %multiply_convert_fusion.1 = (bf16[1024,192]{0,1:T(8,128)(2,1)S(1)}, bf16[1024,192]{0,1:T(8,128)(2,1)S(1)}) fusion(f32[1024,192]{0,1:T(8,128)} %fusion.6, f32[1024,192]{0,1:T(8,128)} %fusion.9, bf16[1024,4096]{1,0:T(8,128)(2,1)} %all-gather.3.cloned.1.call-done, bf16[1,192,4096]{2,1,0:T(8,128)(2,1)S(1)} %copy-done), kind=kOutput, calls=%fused_computation.35 | convolution fusion | flops 1613168640 | bytes 12320768 | tf_op jit(solution)/shard_map/dot_general | solution.py:61
  155.5 8.1 %fusion.4 = f32[1024,4096]{1,0:T(8,128)} fusion(bf16[1024,192]{0,1:T(8,128)(2,1)S(1)} %get-tuple-element.6, bf16[1,2,192,4096]{3,2,1,0:T(8,128)(2,1)S(1)} %copy-done.6), kind=kOutput, calls=%fused_computation.17 | convolution fusion | flops 1610612736 | bytes 18743296 | tf_op jit(solution)/shard_map/dot_general | solution.py:64
  163.6 11.4 %add_convert_fusion = bf16[1024,4096]{1,0:T(8,128)(2,1)} fusion(f32[1024,4096]{1,0:T(8,128)} %fusion.4, bf16[1024,192]{0,1:T(8,128)(2,1)S(1)} %get-tuple-element.5, bf16[1,2,192,4096]{3,2,1,0:T(8,128)(2,1)S(1)} %copy-done.6), kind=kOutput, calls=%fused_computation.5 | convolution fusion | flops 1619001344 | bytes 27131904 | tf_op jit(solution)/shard_map/dot_general | solution.py:65
  175.1 5.6 %fusion.1 = bf16[1,1,192,4096]{3,2,1,0:T(8,128)(2,1)S(1)} fusion(bf16[1024,192]{0,1:T(8,128)(2,1)S(1)} %get-tuple-element.5, bf16[1024,4096]{1,0:T(8,128)(2,1)} %all-gather.5.cloned.1.call-done), kind=kOutput, calls=%fused_computation.11 | convolution fusion | flops 1611399168 | bytes 10354688 | tf_op jit(solution)/shard_map/dot_general | solution.py:81
  180.7 5.4 %fusion = bf16[1,1,192,4096]{3,2,1,0:T(8,128)(2,1)S(1)} fusion(bf16[1024,192]{0,1:T(8,128)(2,1)S(1)} %get-tuple-element.6, bf16[1024,4096]{1,0:T(8,128)(2,1)} %all-gather.5.cloned.1.call-done), kind=kOutput, calls=%fused_computation.10 | convolution fusion | flops 1611399168 | bytes 10354688 | tf_op jit(solution)/shard_map/dot_general | solution.py:80
  186.1 1.9 pad_maximum_fusion
  188.1 0.3 copy-done.4
  188.4 3.0 collective-permute-start
  191.4 1.8 fusion.2
  193.2 0.6 collective-permute-start.1
  193.9 100.4 %collective-permute-done.1 = bf16[1,192,4096]{2,1,0:T(8,128)(2,1)S(1)} collective-permute-done((bf16[1,192,4096]{2,1,0:T(8,128)(2,1)S(1)}, bf16[1,192,4096]{2,1,0:T(8,128)(2,1)S(1)}, u32[]{:S(2)}, u32[]{:S(2)}) %collective-permute-start.1) | collective-permute-done | bytes 1572896 | tf_op jit(solution)/shard_map/ppermute | solution.py:14
  294.3 1.7 add_convert_fusion.2
  295.9 6.8 %all-to-all-start.2 = ((bf16[16,64,512]{2,1,0:T(8,128)(2,1)}), bf16[16,64,512]{2,1,0:T(8,128)(2,1)S(1)}, u32[]{:S(2)}, u32[]{:S(2)}) async-start(bf16[16,64,512]{2,1,0:T(8,128)(2,1)} %reduce-scatter.2.cloned.1.call-done), calls=%async_computation.3 | async-start | bytes 2097152 | tf_op jit(solution)/shard_map/all_to_all | solution.py:72
  302.7 5.3 %add_convert_fusion.1 = bf16[1,2,192,4096]{3,2,1,0:T(8,128)(2,1)} fusion(bf16[1,2,192,4096]{3,2,1,0:T(8,128)(2,1)} %collective-permute-done, bf16[1,1,192,4096]{3,2,1,0:T(8,128)(2,1)S(1)} %fusion.1, bf16[1,1,192,4096]{3,2,1,0:T(8,128)(2,1)} %copy-done.4), kind=kLoop, calls=%fused_computation.6 | loop fusion | flops 7864320 | bytes 9437184 | tf_op jit(solution)/shard_map/convert_element_type | solution.py:89
  308.1 11.8 %all-to-all-done.2 = bf16[16,64,512]{2,1,0:T(8,128)(2,1)S(1)} async-done(((bf16[16,64,512]{2,1,0:T(8,128)(2,1)}), bf16[16,64,512]{2,1,0:T(8,128)(2,1)S(1)}, u32[]{:S(2)}, u32[]{:S(2)}) %all-to-all-start.2) | async-done | bytes 1048608 | tf_op jit(solution)/shard_map/all_to_all | solution.py:72
  319.9 2.0 gather_fusion.3
  322.0 1.3 reduce_sum.25
  (45 shorter events, 1.4 us)
Async XLA Ops:
  7.2 141.3 %copy-start = (bf16[1,192,4096]{2,1,0:T(8,128)(2,1)S(1)}, bf16[1,192,4096]{2,1,0:T(8,128)(2,1)}, u32[]{:S(2)}) copy-start(bf16[1,192,4096]{2,1,0:T(8,128)(2,1)} %param.11) | copy-start | bytes 4718596
  7.2 12.6 %copy-start.2 = (bf16[128,512]{1,0:T(8,128)(2,1)S(1)}, bf16[128,512]{1,0:T(8,128)(2,1)}, u32[]{:S(2)}) copy-start(bf16[128,512]{1,0:T(8,128)(2,1)} %param.6) | copy-start | bytes 393220
  7.2 89.7 %all-gather.5.cloned.1.call-start = ((), (), s32[]{:S(2)}) async-start(), calls=%async_computation.5 | async-start | bytes 9437184 | tf_op jit(solution)/shard_map/all_gather | solution.py:49
  23.7 25.1 %copy-start.3 = (bf16[128,512]{1,0:T(8,128)(2,1)S(1)}, bf16[128,512]{1,0:T(8,128)(2,1)}, u32[]{:S(2)}) copy-start(bf16[128,512]{1,0:T(8,128)(2,1)} %param.7) | copy-start | bytes 393220
  48.7 99.8 %all-gather.3.cloned.1.call-start = ((), (), s32[]{:S(2)}) async-start(), calls=%async_computation.4 | async-start | bytes 9437184 | tf_op jit(solution)/shard_map/all_gather | solution.py:50
  72.8 223.2 %reduce-scatter.2.cloned.1.call-start = ((), (), s32[]{:S(2)}) async-start(), calls=%async_computation.6 | async-start | bytes 9437184 | tf_op jit(solution)/shard_map/reduce_scatter | solution.py:66
  96.9 7.7 %copy-start.5 = (bf16[1,2,192,4096]{3,2,1,0:T(8,128)(2,1)S(1)}, bf16[1,2,192,4096]{3,2,1,0:T(8,128)(2,1)}, u32[]{:S(2)}) copy-start(bf16[1,2,192,4096]{3,2,1,0:T(8,128)(2,1)} %param.10) | copy-start | bytes 9437188
  96.9 7.7 %copy-start.7 = (bf16[1024,4096]{1,0:T(8,128)(2,1)S(1)}, bf16[1024,4096]{1,0:T(8,128)(2,1)}, u32[]{:S(2)}) copy-start(bf16[1024,4096]{1,0:T(8,128)(2,1)} %all-gather.5.cloned.1.call-done) | copy-start | bytes 25165828
  148.5 7.0 %copy-start.6 = (bf16[1,2,192,4096]{3,2,1,0:T(8,128)(2,1)S(1)}, bf16[1,2,192,4096]{3,2,1,0:T(8,128)(2,1)}, u32[]{:S(2)}) copy-start(bf16[1,2,192,4096]{3,2,1,0:T(8,128)(2,1)} %param.10) | copy-start | bytes 9437188
  175.1 16.3 %slice-start = ((s8[8388608]{0:T(1024)(128)(4,1)}), s8[4194304]{0:T(1024)(128)(4,1)S(1)}, s32[]{:S(2)}) async-start(s8[8388608]{0:T(1024)(128)(4,1)} %bitcast.50), calls=%async_computation.7 | async-start | bytes 8388608
  180.7 10.7 %slice-start.1 = ((s8[8388608]{0:T(1024)(128)(4,1)}), s8[4194304]{0:T(1024)(128)(4,1)S(1)}, s32[]{:S(2)}) async-start(s8[8388608]{0:T(1024)(128)(4,1)} %bitcast.50), calls=%async_computation.8 | async-start | bytes 8388608
  186.1 2.3 copy-start.4
  186.1 5.3 %copy-start.8 = (f32[1024,192]{0,1:T(8,128)S(1)}, f32[1024,192]{0,1:T(8,128)}, u32[]{:S(2)}) copy-start(f32[1024,192]{0,1:T(8,128)} %fusion.6) | copy-start | bytes 2359300
  186.1 5.3 %copy-start.9 = (f32[1024,192]{0,1:T(8,128)S(1)}, f32[1024,192]{0,1:T(8,128)}, u32[]{:S(2)}) copy-start(f32[1024,192]{0,1:T(8,128)} %fusion.9) | copy-start | bytes 2359300
  188.4 114.4 %collective-permute-start = (bf16[1,2,192,4096]{3,2,1,0:T(8,128)(2,1)}, bf16[1,2,192,4096]{3,2,1,0:T(8,128)(2,1)}, u32[]{:S(2)}, u32[]{:S(2)}) collective-permute-start(bf16[1,2,192,4096]{3,2,1,0:T(8,128)(2,1)} %pad_maximum_fusion), channel_id=1, source_target_pairs={{0,64},{64,0},{8,72},{72,8},{16,80},{80,16},{24,88},{88,24},{32,96... | collective-permute-start | bytes 9437192 | tf_op jit(solution)/shard_map/ppermute | solution.py:14
  193.2 101.0 %collective-permute-start.1 = (bf16[1,192,4096]{2,1,0:T(8,128)(2,1)S(1)}, bf16[1,192,4096]{2,1,0:T(8,128)(2,1)S(1)}, u32[]{:S(2)}, u32[]{:S(2)}) collective-permute-start(bf16[1,192,4096]{2,1,0:T(8,128)(2,1)S(1)} %fusion.2), channel_id=1, source_target_pairs={{0,64},{64,0},{8,72},{72,8},{16,80},{80,16},{24,88},{88,24},{32,96... | collective-permute-start | bytes 4718600 | tf_op jit(solution)/shard_map/ppermute | solution.py:14
  295.9 23.9 %all-to-all-start.2 = ((bf16[16,64,512]{2,1,0:T(8,128)(2,1)}), bf16[16,64,512]{2,1,0:T(8,128)(2,1)S(1)}, u32[]{:S(2)}, u32[]{:S(2)}) async-start(bf16[16,64,512]{2,1,0:T(8,128)(2,1)} %reduce-scatter.2.cloned.1.call-done), calls=%async_computation.3 | async-start | bytes 2097152 | tf_op jit(solution)/shard_map/all_to_all | solution.py:72
  319.9 3.4 %copy-start.1 = (bf16[1,192,4096]{2,1,0:T(8,128)(2,1)S(1)}, bf16[1,192,4096]{2,1,0:T(8,128)(2,1)}, u32[]{:S(2)}) copy-start(bf16[1,192,4096]{2,1,0:T(8,128)(2,1)} %param.11) | copy-start | bytes 4718596
Sparse Core Ops, SparseCore 0:
  48.8 48.0 all-gather.4
  98.6 49.8 all-gather.2
  175.2 52.6 reduce-scatter.1

commit v2 on v1

v2 whole, which is shorter than its diff:
```python
import functools

import jax
import jax.numpy as jnp
from jax import lax
from jax.experimental import pallas as pl
from jax.experimental.pallas import tpu as pltpu
from jax.sharding import PartitionSpec as P

BF16 = jnp.bfloat16
F32 = jnp.float32
LAST = (((1,), (1,)), ((), ()))
FIRST = (((0,), (0,)), ((), ()))
ROWS = (((1,), (0,)), ((), ()))


def dot(a, b, dims):
    return lax.dot_general(a, b, dims, preferred_element_type=F32)


def kernel(
    n_ep,
    n_y,
    tok,
    og,
    routes,
    probs,
    w_in,
    w_out,
    in_grad,
    grad_in,
    grad_out,
    xs,
    gs,
    wi,
    wo,
    pack_x,
    pack_g,
    onehot,
    named,
    rank,
    share,
    ab,
    dh,
    hid,
    dadb_t,
    dadb,
    own_out,
    rec_out,
    own_in,
    rec_in,
    part_sib,
    part_rec,
    part,
    half_rec,
    full_rec,
    back,
    w_sem,
    a_send,
    a_recv,
    ring_send,
    core_send,
    g_recv,
    eo_send,
    eo_recv,
    ei_send,
    ei_recv,
    p_send,
    p_recv,
    h_send,
    h_recv,
    f_send,
    f_recv,
    b_send,
    b_recv,
    o_sem,
):
    rows, width = xs.shape[1], xs.shape[2]
    cap = rows // n_ep
    half = rows // 2
    ntok = tok.shape[0]
    ff = wo.shape[0]
    tile = min(256, rows)
    lane = min(128, rows)
    wide = min(256, width)
    e = lax.axis_index("ep")
    t = lax.axis_index("tp")
    y = t // 2
    core = t % 2
    sib = y * 2 + (1 - core)
    y_up = lax.rem(y + 1, n_y)
    y_far = lax.rem(y + 2, n_y)
    y_dn = lax.rem(y + n_y - 1, n_y)
    up, far, dn = (v * 2 + core for v in (y_up, y_far, y_dn))
    sup, sfar, sdn = (v * 2 + (1 - core) for v in (y_up, y_far, y_dn))
    other = lax.rem(e + n_ep // 2, n_ep)

    def remote(src, dst, send, recv, ep, tp):
        return pltpu.make_async_remote_copy(
            src_ref=src,
            dst_ref=dst,
            send_sem=send,
            recv_sem=recv,
            device_id=(ep, tp),
            device_id_type=pl.DeviceIdType.MESH,
        )

    def peer(r):
        return lax.rem(e + r, n_ep)

    load_wi = pltpu.make_async_copy(w_in, wi, w_sem.at[0])
    load_wo = pltpu.make_async_copy(w_out, wo, w_sem.at[1])
    load_wi.start()
    load_wo.start()

    barrier = pltpu.get_barrier_semaphore()

    def greet(r, c):
        pl.semaphore_signal(
            barrier, inc=1, device_id=(peer(r), t), device_id_type=pl.DeviceIdType.MESH
        )
        return c

    lax.fori_loop(1, n_ep, greet, 0)
    for who in (sib, up, dn):
        pl.semaphore_signal(barrier, inc=1, device_id=(e, who), device_id_type=pl.DeviceIdType.MESH)

    copy_ids = lax.broadcasted_iota(jnp.int32, (n_ep, ntok), 0)
    hits = jnp.zeros((n_ep, ntok), F32)
    weights = jnp.zeros((n_ep, ntok), F32)
    for k in range(routes.shape[0]):
        same = routes[k : k + 1, :] == copy_ids
        hits = jnp.where(same, 1.0, hits)
        weights = jnp.where(same, probs[k : k + 1, :], weights)
    before = (
        lax.broadcasted_iota(jnp.int32, (ntok, ntok), 0)
        < lax.broadcasted_iota(jnp.int32, (ntok, ntok), 1)
    )
    before = jnp.where(before, 1.0, 0.0).astype(BF16)
    named[...] = hits
    rank[...] = dot(hits.astype(BF16), before, ROWS)
    share[...] = weights
    slots = lax.broadcasted_iota(jnp.int32, (cap, ntok), 0).astype(F32)

    def place(c):
        mine = (named[pl.ds(c, 1), :] > 0.5) & (rank[pl.ds(c, 1), :] == slots)
        return jnp.where(mine, 1.0, 0.0)

    def block(c):
        return pl.ds(pl.multiple_of(c * cap, cap), cap)

    def rows_x(c):
        hot = place(c).astype(BF16)
        onehot[block(c), :] = hot
        return dot(hot, tok[...], ROWS).astype(BF16)

    def rows_g(c):
        hot = place(c)
        scale = jnp.sum(hot * share[pl.ds(c, 1), :], axis=1, keepdims=True)
        return (dot(hot.astype(BF16), og[...], ROWS) * scale).astype(BF16)

    pl.semaphore_wait(barrier, n_ep - 1 + 3)

    def dispatch(which, rows_of, pack, buf):
        def one(r, c):
            j = peer(r)
            pack[j] = rows_of(j)
            remote(
                pack.at[j], buf.at[t, block(e)], a_send.at[which, j], a_recv.at[which, e], j, t
            ).start()
            return c

        lax.fori_loop(1, n_ep, one, 0)
        buf[t, block(e), :] = rows_of(e)

    dispatch(0, rows_x, pack_x, xs)
    dispatch(1, rows_g, pack_g, gs)

    def arrived(which, pack, buf):
        def one(r, c):
            j = peer(r)
            remote(
                pack.at[j], buf.at[t, block(j)], a_send.at[which, j], a_recv.at[which, j], j, t
            ).wait_recv()
            return c

        lax.fori_loop(1, n_ep, one, 0)

    def unit(which, slot, h, send, to):
        buf = (xs, gs)[which]
        ref = buf.at[slot, pl.ds(h * half, half)]
        return remote(ref, ref, send, g_recv.at[which, slot, h], e, to)

    def to_up(which, n, slot, h):
        return unit(which, slot, h, ring_send.at[which, 0, n], up)

    def to_dn(which, n, slot, h):
        return unit(which, slot, h, ring_send.at[which, 1, n], dn)

    def to_sib(which, n, slot, h):
        return unit(which, slot, h, core_send.at[which, n, h], sib)

    def got(which, slot, h):
        unit(which, slot, h, core_send.at[which, 0, h], sib).wait_recv()

    def first_hop(which):
        to_up(which, 0, t, 0).start()
        to_dn(which, 0, t, 1).start()
        to_sib(which, 0, t, 0).start()
        to_sib(which, 0, t, 1).start()
        to_up(which, 1, t, 1).start()
        to_dn(which, 1, t, 0).start()

    def near(which, use):
        use(t)
        got(which, dn, 0)
        to_up(which, 2, dn, 0).start()
        to_sib(which, 1, dn, 0).start()
        got(which, up, 1)
        to_dn(which, 2, up, 1).start()
        to_sib(which, 2, up, 1).start()
        got(which, dn, 1)
        to_sib(which, 1, dn, 1).start()
        use(dn)
        got(which, up, 0)
        to_sib(which, 2, up, 0).start()
        use(up)

    def rest(which, use):
        for slot in (sib, sdn, sup):
            got(which, slot, 0)
            got(which, slot, 1)
            use(slot)
        got(which, far, 0)
        to_sib(which, 3, far, 0).start()
        got(which, far, 1)
        to_sib(which, 3, far, 1).start()
        use(far)
        got(which, sfar, 0)
        got(which, sfar, 1)
        use(sfar)

    def sent(which):
        for n in range(3):
            to_up(which, n, t, 0).wait_send()
            to_dn(which, n, t, 0).wait_send()
        for n in range(4):
            for h in range(2):
                to_sib(which, n, t, h).wait_send()

    def columns(slot):
        return pl.ds(pl.multiple_of(slot * width, width), width)

    def use_x(slot):
        def one(i, c):
            r = pl.ds(pl.multiple_of(i * tile, tile), tile)
            ab[:, r] += dot(wi[:, columns(slot)], xs[slot, r, :], LAST)
            return c

        lax.fori_loop(0, rows // tile, one, 0)

    def send_out(slot):
        return remote(
            own_out.at[slot], rec_out.at[slot], eo_send.at[slot], eo_recv.at[slot], other, t
        )

    def send_in(slot):
        return remote(own_in.at[slot], rec_in.at[slot], ei_send.at[slot], ei_recv.at[slot], other, t)

    def use_g(slot):
        def wgrad(i, c):
            w = pl.ds(pl.multiple_of(i * wide, wide), wide)
            own_out[slot, :, w] = dot(hid[...], gs[slot, :, w], ROWS).astype(BF16)
            return c

        lax.fori_loop(0, width // wide, wgrad, 0)
        send_out(slot).start()

        def one(i, c):
            r = pl.ds(pl.multiple_of(i * tile, tile), tile)
            dh[:, r] += dot(wo[:, columns(slot)], gs[slot, r, :], LAST)
            return c

        lax.fori_loop(0, rows // tile, one, 0)

    ab[...] = jnp.zeros_like(ab)
    dh[...] = jnp.zeros_like(dh)
    load_wi.wait()
    load_wo.wait()
    arrived(0, pack_x, xs)
    first_hop(0)
    near(0, use_x)
    arrived(1, pack_g, gs)
    first_hop(1)
    rest(0, use_x)

    def act(i, c):
        r = pl.ds(pl.multiple_of(i * lane, lane), lane)
        a, b = ab[0:ff, r], ab[ff : 2 * ff, r]
        hid[:, r] = (a * jax.nn.sigmoid(a) * b).astype(BF16)
        return c

    lax.fori_loop(0, rows // lane, act, 0)
    near(1, use_g)
    rest(1, use_g)

    def act_grad(i, c):
        r = pl.ds(pl.multiple_of(i * lane, lane), lane)
        a, b, d = ab[0:ff, r], ab[ff : 2 * ff, r], dh[:, r]
        s = jax.nn.sigmoid(a)
        da = d * b * s * (1.0 + a * (1.0 - s))
        db = d * (a * s)
        dadb_t[0:ff, r] = da.astype(BF16)
        dadb_t[ff : 2 * ff, r] = db.astype(BF16)
        dadb[r, :] = jnp.concatenate([da, db], axis=0).T.astype(BF16)
        return c

    lax.fori_loop(0, rows // lane, act_grad, 0)

    def wgrad_in(slot):
        def one(i, c):
            w = pl.ds(pl.multiple_of(i * wide, wide), wide)
            own_in[slot, :, w] = dot(dadb_t[...], xs[slot, :, w], ROWS).astype(BF16)
            return c

        lax.fori_loop(0, width // wide, one, 0)
        send_in(slot).start()

    def term(slot, dst, at):
        def one(i, c):
            r = pl.ds(pl.multiple_of(i * tile, tile), tile)
            dst[at, r, :] = dot(dadb[r, :], wi[:, columns(slot)], ROWS).astype(BF16)
            return c

        lax.fori_loop(0, rows // tile, one, 0)

    def send_part(at):
        return remote(part_sib.at[at], part_rec.at[at], p_send.at[at], p_recv.at[at], e, sib)

    for i, (yd, slot) in enumerate(((y_far, sfar), (y_up, sup), (y_dn, sdn), (y, sib))):
        wgrad_in(i)
        term(slot, part_sib, yd)
        send_part(yd).start()
    for i, (yd, slot) in enumerate(((y_far, far), (y_up, up), (y_dn, dn), (y, t))):
        wgrad_in(4 + i)
        term(slot, part, yd)

    def add(ref, at, src, src_at, h):
        r = pl.ds(h * half, half)
        ref[at, r, :] = (ref[at, r, :].astype(F32) + src[src_at, r, :].astype(F32)).astype(BF16)

    def chip(at):
        send_part(at).wait_recv()
        for h in range(2):
            add(part, at, part_rec, at, h)

    lower, upper = pl.ds(0, half), pl.ds(half, half)
    far_dn = remote(
        part.at[y_far, lower], half_rec.at[0, lower], h_send.at[0], h_recv.at[0], e, dn
    )
    far_up = remote(
        part.at[y_far, upper], half_rec.at[0, upper], h_send.at[1], h_recv.at[1], e, up
    )

    def full(direction, h):
        r = (lower, upper)[h]
        at, to = ((y_dn, dn), (y_up, up))[direction]
        return remote(
            part.at[at, r],
            full_rec.at[direction, r],
            f_send.at[direction, h],
            f_recv.at[direction, h],
            e,
            to,
        )

    chip(y_far)
    far_dn.start()
    far_up.start()
    chip(y_dn)
    full(0, 1).start()
    chip(y_up)
    full(1, 0).start()
    far_dn.wait_recv()
    add(part, y_dn, half_rec, 0, 0)
    full(0, 0).start()
    far_up.wait_recv()
    add(part, y_up, half_rec, 0, 1)
    full(1, 1).start()
    send_part(y).wait_recv()

    for h in range(2):
        full(0, h).wait_recv()
        full(1, h).wait_recv()

    def total(i, c):
        r = block(i)
        mine = part[y, r, :].astype(F32) + part_rec[y, r, :].astype(F32)
        ring = full_rec[0, r, :].astype(F32) + full_rec[1, r, :].astype(F32)
        part[y, r, :] = (mine + ring).astype(BF16)
        return c

    lax.fori_loop(0, n_ep, total, 0)

    def home(j, at):
        return remote(part.at[y, block(j)], back.at[block(at)], b_send.at[j], b_recv.at[at], j, t)

    def send_home(r, c):
        home(peer(r), e).start()
        return c

    lax.fori_loop(1, n_ep, send_home, 0)
    back[block(e), :] = part[y, block(e), :]

    def got_home(r, c):
        home(peer(r), peer(r)).wait_recv()
        return c

    lax.fori_loop(1, n_ep, got_home, 0)
    in_grad[...] = dot(onehot[...], back[...], FIRST).astype(BF16)

    def store_out(slot):
        return pltpu.make_async_copy(
            rec_out.at[slot], grad_out.at[:, columns(slot)], o_sem.at[0, slot]
        )

    def store_in(slot):
        return pltpu.make_async_copy(rec_in.at[slot], grad_in.at[:, columns(slot)], o_sem.at[1, slot])

    for slot in (t, dn, up, sib, sdn, sup, far, sfar):
        send_out(slot).wait_recv()
        rec_out[slot] = (rec_out[slot].astype(F32) + own_out[slot].astype(F32)).astype(BF16)
        store_out(slot).start()

    def merge(slot, c):
        send_in(slot).wait_recv()
        rec_in[slot] = (rec_in[slot].astype(F32) + own_in[slot].astype(F32)).astype(BF16)
        store_in(slot).start()
        return c

    lax.fori_loop(0, 2 * n_y, merge, 0)

    def end_peers(r, c):
        j = peer(r)
        for which, pack in ((0, pack_x), (1, pack_g)):
            remote(
                pack.at[j], pack.at[j], a_send.at[which, j], a_recv.at[which, j], j, t
            ).wait_send()
        home(j, e).wait_send()
        return c

    lax.fori_loop(1, n_ep, end_peers, 0)
    sent(0)
    sent(1)
    far_dn.wait_send()
    far_up.wait_send()
    for direction in range(2):
        for h in range(2):
            full(direction, h).wait_send()

    def end_parts(at, c):
        send_part(at).wait_send()
        return c

    lax.fori_loop(0, n_y, end_parts, 0)

    def end_grads(slot, c):
        send_out(slot).wait_send()
        send_in(slot).wait_send()
        store_out(slot).wait()
        store_in(slot).wait()
        return c

    lax.fori_loop(0, 2 * n_y, end_grads, 0)


def body(tokens, out_grad, routes, probs, w_in, w_out):
    n_ep = lax.axis_size("ep")
    n_tp = lax.axis_size("tp")
    n_y = n_tp // 2
    ntok, top = routes.shape
    cap = 2 * ntok * top // n_ep
    rows = n_ep * cap
    width = tokens.shape[1]
    ff = w_out.shape[1]
    depth = w_out.shape[2]
    half = rows // 2
    dma = pltpu.SemaphoreType.DMA
    vmem = pl.BlockSpec(memory_space=pltpu.VMEM)
    anywhere = pl.BlockSpec(memory_space=pl.ANY)
    flops = 2 * rows * depth * ff * 8
    in_grad, grad_in, grad_out = pl.pallas_call(
        functools.partial(kernel, n_ep, n_y),
        out_shape=(
            jax.ShapeDtypeStruct((ntok, width), BF16),
            jax.ShapeDtypeStruct((2 * ff, depth), BF16),
            jax.ShapeDtypeStruct((ff, depth), BF16),
        ),
        in_specs=[vmem, vmem, vmem, vmem, anywhere, anywhere],
        out_specs=(vmem, anywhere, anywhere),
        scratch_shapes=[
            pltpu.VMEM((n_tp, rows, width), BF16),
            pltpu.VMEM((n_tp, rows, width), BF16),
            pltpu.VMEM((2 * ff, depth), BF16),
            pltpu.VMEM((ff, depth), BF16),
            pltpu.VMEM((n_ep, cap, width), BF16),
            pltpu.VMEM((n_ep, cap, width), BF16),
            pltpu.VMEM((rows, ntok), BF16),
            pltpu.VMEM((n_ep, ntok), F32),
            pltpu.VMEM((n_ep, ntok), F32),
            pltpu.VMEM((n_ep, ntok), F32),
            pltpu.VMEM((2 * ff, rows), F32),
            pltpu.VMEM((ff, rows), F32),
            pltpu.VMEM((ff, rows), BF16),
            pltpu.VMEM((2 * ff, rows), BF16),
            pltpu.VMEM((rows, 2 * ff), BF16),
            pltpu.VMEM((n_tp, ff, width), BF16),
            pltpu.VMEM((n_tp, ff, width), BF16),
            pltpu.VMEM((n_tp, 2 * ff, width), BF16),
            pltpu.VMEM((n_tp, 2 * ff, width), BF16),
            pltpu.VMEM((n_y, rows, width), BF16),
            pltpu.VMEM((n_y, rows, width), BF16),
            pltpu.VMEM((n_y, rows, width), BF16),
            pltpu.VMEM((1, rows, width), BF16),
            pltpu.VMEM((2, rows, width), BF16),
            pltpu.VMEM((rows, width), BF16),
            dma((2,)),
            dma((2, n_ep)),
            dma((2, n_ep)),
            dma((2, 2, 3)),
            dma((2, 4, 2)),
            dma((2, n_tp, 2)),
            dma((n_tp,)),
            dma((n_tp,)),
            dma((n_tp,)),
            dma((n_tp,)),
            dma((n_y,)),
            dma((n_y,)),
            dma((2,)),
            dma((2,)),
            dma((2, 2)),
            dma((2, 2)),
            dma((n_ep,)),
            dma((n_ep,)),
            dma((2, n_tp)),
        ],
        compiler_params=pltpu.CompilerParams(
            collective_id=0, has_side_effects=True, vmem_limit_bytes=60 * 1024 * 1024
        ),
        cost_estimate=pl.CostEstimate(
            flops=flops, bytes_accessed=4 * rows * depth, transcendentals=2 * rows * ff
        ),
    )(
        tokens,
        out_grad,
        routes.T,
        probs.astype(F32).T,
        w_in.reshape(2 * ff, depth),
        w_out.reshape(ff, depth),
    )
    return in_grad, grad_in.reshape(1, 2, ff, depth), grad_out.reshape(1, ff, depth)


def solution(mesh):
    return jax.shard_map(
        body,
        mesh=mesh,
        in_specs=(
            P("ep", "tp"),
            P("ep", "tp"),
            P("ep", None),
            P("ep", None),
            P("ep", None, "tp", None),
            P("ep", "tp", None),
        ),
        out_specs=(P("ep", "tp"), P("ep", None, "tp", None), P("ep", "tp", None)),
        check_vma=False,
    )
```

time: 330 us -> 212 us (0.64)
  Pallas kernels: 0 us -> 202 us
  waiting for transfers between devices: 176 us -> 0 us
  matrix products: 50.8 us -> 0 us
  blocking collectives: 44.4 us -> 0 us
  local copies, waits for them, and re-layouts: 21.8 us -> 6.74 us
  between operations: 14 us -> 0.64 us
  starting transfers between devices: 10.7 us -> 0 us
  other arithmetic: 11.9 us -> 1.26 us
    pallas_call x0 -> x1, Pallas kernels: none -> 202 us  [body(): pl.pallas_call(functools.partial(kernel, n_ep, n_y), out_shape=(jax.Shape...]
    ppermute x2 -> x0, waiting for transfers between devices: 100 us -> none  [partner(): return lax.ppermute(block, axis, route)]
    all_gather x2 -> x0, waiting for transfers between devices: 64 us -> none  [the longest x1 40.1 us: body(): lax.all_gather(recv_g.reshape(n_ep * cap, part), 'tp', axis=1, tiled=True)]
    dot_general x8 -> x0, matrix products: 50.8 us -> none  [the longest x1 11.4 us: body(): jnp.dot(db, w_up, preferred_element_type=jnp.float32)]
    all_to_all x2 -> x0, blocking collectives: 44.4 us -> none  [the longest x1 24.7 us: body(): lax.all_to_all(send_x, 'ep', split_axis=0, concat_axis=0, tiled=True)]
    gather x5 -> x0, local copies, waits for them, and re-layouts: 16.8 us -> none  [the longest x1 6.8 us: body(): probs.reshape(-1)[local].astype(jnp.float32)]
    all_to_all x1 -> x0, waiting for transfers between devices: 11.8 us -> none  [body(): back = lax.all_to_all(summed, 'ep', split_axis=0, concat_axis=0, tiled=True)]
    convert_element_type x3 -> x0, other arithmetic: 7.3 us -> none  [the longest x1 5.32 us: body(): (own_in.astype(jnp.float32) + other_in.astype(jnp.float32)).astype(jnp.bf...]
  transfers between devices with their start and end apart: 6 -> 0, of which waited for: 4 -> 0; matrix products, arithmetic and copies ran while one was open for 11% -> 0% of each run, Pallas kernels for 0% -> 0%
where the time goes in v2:
time: 212 us; the launch traced here: 211 us
  Pallas kernels  202 us (95%)
  local copies, waits for them, and re-layouts  6.74 us (3%)
    pallas_call x1, Pallas kernels, body(): pl.pallas_call(functools.partial(kernel, n_ep, n_y), out_shape=(jax.Shape...  202 us
    unnamed x5, local copies, waits for them, and re-layouts  6.74 us

profile of v2, /device:TPU:0, one launch (start us, length us, event | category | flops | bytes accessed | tf_op | source)
XLA Modules:
  0.0 210.8 jit_solution(16964565661677163848)
XLA Ops:
  0.6 1.3 convert_bitcast_fusion.probs
  1.9 202.2 %shard_map.85 = (bf16[128,512]{1,0:T(8,128)(2,1)}, bf16[384,4096]{1,0:T(8,128)(2,1)}, bf16[192,4096]{1,0:T(8,128)(2,1)}) custom-call(bf16[128,512]{1,0:T(8,128)(2,1)} %tok.1, bf16[128,512]{1,0:T(8,128)(2,1)} %og.1, s32[4,128]{1,0:T(4,128)} %bitcast.11, f32[4,128]{1,0:T(4,128)} %convert_bitcast_fusion.probs, bf16[384,4096]{1,0:T(8,128)(2,1)} %bitcast.9, ...), custom_call_target="tpu_custom_call" | custom-call | flops 12884901888 | bytes 16777216 | tf_op jit(solution)/shard_map/pallas_call | solution.py:492
  204.1 1.6 copy.12
  205.7 0.0 copy-start
  205.7 4.0 %copy.13 = bf16[1,2,192,4096]{3,2,1,0:T(8,128)(2,1)} copy(bf16[1,2,192,4096]{3,2,1,0:T(8,128)(2,1)} %bitcast.7) | data formatting | bytes 6291456
  209.7 0.0 copy-done
  209.7 1.1 copy.14
Async XLA Ops:
  205.7 4.0 %copy-start = (bf16[192,4096]{1,0:T(8,128)(2,1)S(1)}, bf16[192,4096]{1,0:T(8,128)(2,1)}, u32[]{:S(2)}) copy-start(bf16[192,4096]{1,0:T(8,128)(2,1)} %get-tuple-element.8) | copy-start | bytes 4718596

commit v3 on v2

v3 whole, which is shorter than its diff:
```python
import functools

import jax
import jax.numpy as jnp
from jax import lax
from jax.experimental import pallas as pl
from jax.experimental.pallas import tpu as pltpu
from jax.sharding import PartitionSpec as P

BF16 = jnp.bfloat16
F32 = jnp.float32
LAST = (((1,), (1,)), ((), ()))
FIRST = (((0,), (0,)), ((), ()))
ROWS = (((1,), (0,)), ((), ()))


def dot(a, b, dims):
    return lax.dot_general(a, b, dims, preferred_element_type=F32)


def store(in_grad, grad_in, grad_out, in_grad_hbm, grad_in_hbm, grad_out_hbm, sems):
    copies = [
        pltpu.make_async_copy(src, dst, sems.at[i])
        for i, (src, dst) in enumerate(
            ((grad_in, grad_in_hbm), (grad_out, grad_out_hbm), (in_grad, in_grad_hbm))
        )
    ]
    for copy in copies:
        copy.start()
    for copy in copies:
        copy.wait()


def kernel(
    n_ep,
    n_y,
    tok_hbm,
    og_hbm,
    routes,
    probs,
    w_in,
    w_out,
    in_grad,
    grad_in,
    grad_out,
    tok,
    og,
    xs,
    gs,
    wi,
    wo,
    pack_x,
    pack_g,
    onehot,
    named,
    rank,
    share,
    ab,
    dh,
    hid,
    dadb_t,
    dadb,
    own_out,
    own_in,
    part_sib,
    part_rec,
    part,
    half_rec,
    full_rec,
    back,
    load_sem,
    a_send,
    a_recv,
    ring_send,
    core_send,
    g_recv,
    eo_send,
    eo_recv,
    ei_send,
    ei_recv,
    p_send,
    p_recv,
    h_send,
    h_recv,
    f_send,
    f_recv,
    b_send,
    b_recv,
):
    n_unit, rows, uw = xs.shape
    cap = rows // n_ep
    half = rows // 2
    width = tok.shape[1]
    ntok = tok.shape[0]
    ff = wo.shape[0]
    tile = min(256, rows)
    lane = min(128, rows)
    e = lax.axis_index("ep")
    t = lax.axis_index("tp")
    y = t // 2
    core = t % 2
    sib = y * 2 + (1 - core)
    y_up = lax.rem(y + 1, n_y)
    y_far = lax.rem(y + 2, n_y)
    y_dn = lax.rem(y + n_y - 1, n_y)
    up, far, dn = (v * 2 + core for v in (y_up, y_far, y_dn))
    sup, sfar, sdn = (v * 2 + (1 - core) for v in (y_up, y_far, y_dn))
    other = lax.rem(e + n_ep // 2, n_ep)

    def remote(src, dst, send, recv, ep, tp):
        return pltpu.make_async_remote_copy(
            src_ref=src,
            dst_ref=dst,
            send_sem=send,
            recv_sem=recv,
            device_id=(ep, tp),
            device_id_type=pl.DeviceIdType.MESH,
        )

    def peer(r):
        return lax.rem(e + r, n_ep)

    def signal(ep, tp):
        pl.semaphore_signal(
            barrier, inc=1, device_id=(ep, tp), device_id_type=pl.DeviceIdType.MESH
        )

    barrier = pltpu.get_barrier_semaphore()

    def greet(r, c):
        signal(peer(r), t)
        return c

    lax.fori_loop(1, n_ep, greet, 0)
    for who in (sib, up, dn):
        signal(e, who)

    load_tok, load_og, load_wi, load_wo = (
        pltpu.make_async_copy(src, dst, load_sem.at[i])
        for i, (src, dst) in enumerate(((tok_hbm, tok), (og_hbm, og), (w_in, wi), (w_out, wo)))
    )
    load_tok.start()
    load_og.start()
    load_wi.start()
    load_wo.start()

    copy_ids = lax.broadcasted_iota(jnp.int32, (n_ep, ntok), 0)
    hits = jnp.zeros((n_ep, ntok), F32)
    weights = jnp.zeros((n_ep, ntok), F32)
    shares = probs[...].astype(F32)
    for k in range(routes.shape[0]):
        same = routes[k : k + 1, :] == copy_ids
        hits = jnp.where(same, 1.0, hits)
        weights = jnp.where(same, shares[k : k + 1, :], weights)
    before = (
        lax.broadcasted_iota(jnp.int32, (ntok, ntok), 0)
        < lax.broadcasted_iota(jnp.int32, (ntok, ntok), 1)
    )
    before = jnp.where(before, 1.0, 0.0).astype(BF16)
    named[...] = hits
    rank[...] = dot(hits.astype(BF16), before, ROWS)
    share[...] = weights
    slots = lax.broadcasted_iota(jnp.int32, (cap, ntok), 0).astype(F32)

    def place(c):
        mine = (named[pl.ds(c, 1), :] > 0.5) & (rank[pl.ds(c, 1), :] == slots)
        return jnp.where(mine, 1.0, 0.0)

    def block(c):
        return pl.ds(pl.multiple_of(c * cap, cap), cap)

    def rows_x(c):
        hot = place(c).astype(BF16)
        onehot[block(c), :] = hot
        return dot(hot, tok[...], ROWS).astype(BF16)

    def rows_g(c):
        hot = place(c)
        scale = jnp.sum(hot * share[pl.ds(c, 1), :], axis=1, keepdims=True)
        return (dot(hot.astype(BF16), og[...], ROWS) * scale).astype(BF16)

    def pack_rows(rows_of, pack, buf):
        def one(r, c):
            j = peer(r)
            made = rows_of(j)
            for h in range(2):
                pack[j, h] = made[:, h * uw : (h + 1) * uw]
            return c

        lax.fori_loop(1, n_ep, one, 0)
        made = rows_of(e)
        for h in range(2):
            buf[t * 2 + h, block(e), :] = made[:, h * uw : (h + 1) * uw]

    packs, bufs = (pack_x, pack_g), (xs, gs)

    def rows_copy(which, h, j, at):
        return remote(
            packs[which].at[j, h],
            bufs[which].at[t * 2 + h, block(at)],
            a_send.at[which, h, j],
            a_recv.at[which, h, at],
            j,
            t,
        )

    def dispatch(which):
        for h in range(2):

            def one(r, c, h=h):
                rows_copy(which, h, peer(r), e).start()
                return c

            lax.fori_loop(1, n_ep, one, 0)

    def arrived(which, h):
        def one(r, c):
            rows_copy(which, h, peer(r), peer(r)).wait_recv()
            return c

        lax.fori_loop(1, n_ep, one, 0)

    load_tok.wait()
    pack_rows(rows_x, pack_x, xs)
    ab[...] = jnp.zeros_like(ab)
    dh[...] = jnp.zeros_like(dh)
    pl.semaphore_wait(barrier, n_ep - 1 + 3)
    dispatch(0)
    load_og.wait()
    pack_rows(rows_g, pack_g, gs)
    dispatch(1)
    load_wi.wait()
    load_wo.wait()

    def unit(which, slot, h, send, to):
        ref = bufs[which].at[slot * 2 + h]
        return remote(ref, ref, send, g_recv.at[which, slot * 2 + h], e, to)

    def to_up(which, n, slot, h):
        return unit(which, slot, h, ring_send.at[which, 0, n], up)

    def to_dn(which, n, slot, h):
        return unit(which, slot, h, ring_send.at[which, 1, n], dn)

    def to_sib(which, n, slot, h):
        return unit(which, slot, h, core_send.at[which, n, h], sib)

    def got(which, slot, h):
        unit(which, slot, h, core_send.at[which, 0, h], sib).wait_recv()

    def first_hop(which):
        for h in range(2):
            arrived(which, h)
            to_up(which, h, t, h).start()
            to_dn(which, h, t, h).start()
            to_sib(which, 0, t, h).start()

    def gather(which, use, between):
        use(t, 0)
        use(t, 1)
        for h in range(2):
            got(which, sib, h)
            use(sib, h)
        got(which, dn, 0)
        to_up(which, 2, dn, 0).start()
        to_sib(which, 1, dn, 0).start()
        got(which, up, 0)
        to_sib(which, 2, up, 0).start()
        use(dn, 0)
        use(up, 0)
        for slot in (sdn, sup):
            got(which, slot, 0)
            use(slot, 0)
        got(which, up, 1)
        to_dn(which, 2, up, 1).start()
        to_sib(which, 2, up, 1).start()
        got(which, dn, 1)
        to_sib(which, 1, dn, 1).start()
        between()
        use(dn, 1)
        use(up, 1)
        for slot in (sdn, sup):
            got(which, slot, 1)
            use(slot, 1)
        for h in range(2):
            got(which, far, h)
            to_sib(which, 3, far, h).start()
            use(far, h)
        for h in range(2):
            got(which, sfar, h)
            use(sfar, h)

    def sent(which):
        for n in range(3):
            to_up(which, n, t, 0).wait_send()
            to_dn(which, n, t, 0).wait_send()
        for n in range(4):
            for h in range(2):
                to_sib(which, n, t, h).wait_send()

    def columns(slot):
        return pl.ds(pl.multiple_of(slot * width, width), width)

    def ucolumns(u):
        return pl.ds(pl.multiple_of(u * uw, uw), uw)

    def use_x(slot, h):
        u = slot * 2 + h

        def one(i, c):
            r = pl.ds(pl.multiple_of(i * tile, tile), tile)
            ab[:, r] += dot(wi[:, ucolumns(u)], xs[u, r, :], LAST)
            return c

        lax.fori_loop(0, rows // tile, one, 0)

    def send_out(u):
        return remote(
            own_out.at[u], grad_out.at[:, ucolumns(u)], eo_send.at[u], eo_recv.at[u], other, t
        )

    def send_in(u):
        return remote(
            own_in.at[u], grad_in.at[:, ucolumns(u)], ei_send.at[u], ei_recv.at[u], other, t
        )

    def use_g(slot, h):
        u = slot * 2 + h
        own_out[u] = dot(hid[...], gs[u], ROWS).astype(BF16)
        send_out(u).start()

        def one(i, c):
            r = pl.ds(pl.multiple_of(i * tile, tile), tile)
            dh[:, r] += dot(wo[:, ucolumns(u)], gs[u, r, :], LAST)
            return c

        lax.fori_loop(0, rows // tile, one, 0)

    first_hop(0)
    gather(0, use_x, functools.partial(first_hop, 1))

    def act(i, c):
        r = pl.ds(pl.multiple_of(i * lane, lane), lane)
        a, b = ab[0:ff, r], ab[ff : 2 * ff, r]
        hid[:, r] = (a * jax.nn.sigmoid(a) * b).astype(BF16)
        return c

    lax.fori_loop(0, rows // lane, act, 0)
    gather(1, use_g, lambda: None)

    def act_grad(i, c):
        r = pl.ds(pl.multiple_of(i * lane, lane), lane)
        a, b, d = ab[0:ff, r], ab[ff : 2 * ff, r], dh[:, r]
        s = jax.nn.sigmoid(a)
        da = d * b * s * (1.0 + a * (1.0 - s))
        db = d * (a * s)
        dadb_t[0:ff, r] = da.astype(BF16)
        dadb_t[ff : 2 * ff, r] = db.astype(BF16)
        dadb[r, :] = jnp.concatenate([da, db], axis=0).T.astype(BF16)
        return c

    lax.fori_loop(0, rows // lane, act_grad, 0)

    def wgrad_in(u):
        own_in[u] = dot(dadb_t[...], xs[u], ROWS).astype(BF16)
        send_in(u).start()

    def term(slot, dst, at):
        def one(i, c):
            r = pl.ds(pl.multiple_of(i * tile, tile), tile)
            dst[at, r, :] = dot(dadb[r, :], wi[:, columns(slot)], ROWS).astype(BF16)
            return c

        lax.fori_loop(0, rows // tile, one, 0)

    def send_part(at):
        return remote(part_sib.at[at], part_rec.at[at], p_send.at[at], p_recv.at[at], e, sib)

    for i, (yd, slot) in enumerate(((y_far, sfar), (y_up, sup), (y_dn, sdn), (y, sib))):
        wgrad_in(2 * i)
        wgrad_in(2 * i + 1)
        term(slot, part_sib, yd)
        send_part(yd).start()
    for i, (yd, slot) in enumerate(((y_far, far), (y_up, up), (y_dn, dn), (y, t))):
        wgrad_in(8 + 2 * i)
        wgrad_in(9 + 2 * i)
        term(slot, part, yd)

    def add(ref, at, src, src_at, h):
        r = pl.ds(h * half, half)
        ref[at, r, :] = (ref[at, r, :].astype(F32) + src[src_at, r, :].astype(F32)).astype(BF16)

    def chip(at):
        send_part(at).wait_recv()
        for h in range(2):
            add(part, at, part_rec, at, h)

    lower, upper = pl.ds(0, half), pl.ds(half, half)
    far_dn = remote(
        part.at[y_far, lower], half_rec.at[0, lower], h_send.at[0], h_recv.at[0], e, dn
    )
    far_up = remote(
        part.at[y_far, upper], half_rec.at[0, upper], h_send.at[1], h_recv.at[1], e, up
    )

    def full(direction, h):
        r = (lower, upper)[h]
        at, to = ((y_dn, dn), (y_up, up))[direction]
        return remote(
            part.at[at, r],
            full_rec.at[direction, r],
            f_send.at[direction, h],
            f_recv.at[direction, h],
            e,
            to,
        )

    chip(y_far)
    far_dn.start()
    far_up.start()
    chip(y_dn)
    full(0, 1).start()
    chip(y_up)
    full(1, 0).start()
    far_dn.wait_recv()
    add(part, y_dn, half_rec, 0, 0)
    full(0, 0).start()
    far_up.wait_recv()
    add(part, y_up, half_rec, 0, 1)
    full(1, 1).start()
    send_part(y).wait_recv()

    for h in range(2):
        full(0, h).wait_recv()
        full(1, h).wait_recv()

    def total(i, c):
        r = block(i)
        mine = part[y, r, :].astype(F32) + part_rec[y, r, :].astype(F32)
        ring = full_rec[0, r, :].astype(F32) + full_rec[1, r, :].astype(F32)
        part[y, r, :] = (mine + ring).astype(BF16)
        return c

    lax.fori_loop(0, n_ep, total, 0)

    def home(j, at):
        return remote(part.at[y, block(j)], back.at[block(at)], b_send.at[j], b_recv.at[at], j, t)

    def send_home(r, c):
        home(peer(r), e).start()
        return c

    lax.fori_loop(1, n_ep, send_home, 0)
    back[block(e), :] = part[y, block(e), :]

    def merge_out(u, c):
        send_out(u).wait_recv()
        w = ucolumns(u)
        grad_out[:, w] = (grad_out[:, w].astype(F32) + own_out[u].astype(F32)).astype(BF16)
        return c

    lax.fori_loop(0, n_unit, merge_out, 0)

    def got_home(r, c):
        home(peer(r), peer(r)).wait_recv()
        return c

    lax.fori_loop(1, n_ep, got_home, 0)
    in_grad[...] = dot(onehot[...], back[...], FIRST).astype(BF16)

    def merge_in(u, c):
        send_in(u).wait_recv()
        w = ucolumns(u)
        grad_in[:, w] = (grad_in[:, w].astype(F32) + own_in[u].astype(F32)).astype(BF16)
        return c

    lax.fori_loop(0, n_unit, merge_in, 0)

    def end_peers(r, c):
        j = peer(r)
        for which in range(2):
            for h in range(2):
                rows_copy(which, h, j, e).wait_send()
        home(j, e).wait_send()
        return c

    lax.fori_loop(1, n_ep, end_peers, 0)
    sent(0)
    sent(1)
    far_dn.wait_send()
    far_up.wait_send()
    for direction in range(2):
        for h in range(2):
            full(direction, h).wait_send()

    def end_parts(at, c):
        send_part(at).wait_send()
        return c

    lax.fori_loop(0, n_y, end_parts, 0)

    def end_grads(u, c):
        send_out(u).wait_send()
        send_in(u).wait_send()
        return c

    lax.fori_loop(0, n_unit, end_grads, 0)


def body(tokens, out_grad, routes, probs, w_in, w_out):
    n_ep = lax.axis_size("ep")
    n_tp = lax.axis_size("tp")
    n_y = n_tp // 2
    n_unit = 2 * n_tp
    ntok, top = routes.shape
    cap = 2 * ntok * top // n_ep
    rows = n_ep * cap
    width = tokens.shape[1]
    uw = width // 2
    ff = w_out.shape[1]
    depth = w_out.shape[2]
    dma = pltpu.SemaphoreType.DMA
    vmem = pl.BlockSpec(memory_space=pltpu.VMEM)
    anywhere = pl.BlockSpec(memory_space=pl.ANY)
    flops = 2 * rows * depth * ff * 8
    made = pl.pallas_call(
        functools.partial(kernel, n_ep, n_y),
        out_shape=(
            pltpu.VMEM((ntok, width), BF16),
            pltpu.VMEM((2 * ff, depth), BF16),
            pltpu.VMEM((ff, depth), BF16),
        ),
        in_specs=[anywhere, anywhere, vmem, vmem, anywhere, anywhere],
        out_specs=(vmem, vmem, vmem),
        scratch_shapes=[
            pltpu.VMEM((ntok, width), BF16),
            pltpu.VMEM((ntok, width), BF16),
            pltpu.VMEM((n_unit, rows, uw), BF16),
            pltpu.VMEM((n_unit, rows, uw), BF16),
            pltpu.VMEM((2 * ff, depth), BF16),
            pltpu.VMEM((ff, depth), BF16),
            pltpu.VMEM((n_ep, 2, cap, uw), BF16),
            pltpu.VMEM((n_ep, 2, cap, uw), BF16),
            pltpu.VMEM((rows, ntok), BF16),
            pltpu.VMEM((n_ep, ntok), F32),
            pltpu.VMEM((n_ep, ntok), F32),
            pltpu.VMEM((n_ep, ntok), F32),
            pltpu.VMEM((2 * ff, rows), F32),
            pltpu.VMEM((ff, rows), F32),
            pltpu.VMEM((ff, rows), BF16),
            pltpu.VMEM((2 * ff, rows), BF16),
            pltpu.VMEM((rows, 2 * ff), BF16),
            pltpu.VMEM((n_unit, ff, uw), BF16),
            pltpu.VMEM((n_unit, 2 * ff, uw), BF16),
            pltpu.VMEM((n_y, rows, width), BF16),
            pltpu.VMEM((n_y, rows, width), BF16),
            pltpu.VMEM((n_y, rows, width), BF16),
            pltpu.VMEM((1, rows, width), BF16),
            pltpu.VMEM((2, rows, width), BF16),
            pltpu.VMEM((rows, width), BF16),
            dma((4,)),
            dma((2, 2, n_ep)),
            dma((2, 2, n_ep)),
            dma((2, 2, 3)),
            dma((2, 4, 2)),
            dma((2, n_unit)),
            dma((n_unit,)),
            dma((n_unit,)),
            dma((n_unit,)),
            dma((n_unit,)),
            dma((n_y,)),
            dma((n_y,)),
            dma((2,)),
            dma((2,)),
            dma((2, 2)),
            dma((2, 2)),
            dma((n_ep,)),
            dma((n_ep,)),
        ],
        compiler_params=pltpu.CompilerParams(
            collective_id=0, has_side_effects=True, vmem_limit_bytes=56 * 1024 * 1024
        ),
        cost_estimate=pl.CostEstimate(
            flops=flops, bytes_accessed=4 * rows * depth, transcendentals=2 * rows * ff
        ),
    )(
        tokens,
        out_grad,
        routes.T,
        probs.T,
        w_in.reshape(2 * ff, depth),
        w_out.reshape(ff, depth),
    )
    in_grad, grad_in, grad_out = pl.pallas_call(
        store,
        out_shape=tuple(jax.ShapeDtypeStruct(m.shape, BF16) for m in made),
        in_specs=[anywhere] * 3,
        out_specs=(anywhere,) * 3,
        scratch_shapes=[dma((3,))],
        compiler_params=pltpu.CompilerParams(vmem_limit_bytes=1024 * 1024),
    )(*(pltpu.with_memory_space_constraint(m, pltpu.VMEM) for m in made))
    return in_grad, grad_in.reshape(1, 2, ff, depth), grad_out.reshape(1, ff, depth)


def solution(mesh):
    return jax.shard_map(
        body,
        mesh=mesh,
        in_specs=(
            P("ep", "tp"),
            P("ep", "tp"),
            P("ep", None),
            P("ep", None),
            P("ep", None, "tp", None),
            P("ep", "tp", None),
        ),
        out_specs=(P("ep", "tp"), P("ep", None, "tp", None), P("ep", "tp", None)),
        check_vma=False,
    )
```

time: 212 us -> 186 us (0.88)
  Pallas kernels: 202 us -> 183 us
  local copies, waits for them, and re-layouts: 6.74 us -> 0 us
    pallas_call x1 -> x2, Pallas kernels: 202 us -> 183 us  [the longest x1 181 us: body(): pl.pallas_call(functools.partial(kernel, n_ep, n_y), out_shape=(pltpu.VME...]
    unnamed x5 -> x0, local copies, waits for them, and re-layouts: 6.74 us -> none
where the time goes in v3:
time: 186 us; the launch traced here: 183 us
  Pallas kernels  183 us (98%)
    pallas_call x1, Pallas kernels, body(): pl.pallas_call(functools.partial(kernel, n_ep, n_y), out_shape=(pltpu.VME...  181 us

profile of v3, /device:TPU:0, one launch (start us, length us, event | category | flops | bytes accessed | tf_op | source)
XLA Modules:
  0.0 183.4 jit_solution(3381083998277744961)
XLA Ops:
  0.6 180.6 %shard_map.85 = (bf16[128,512]{1,0:T(8,128)(2,1)S(1)}, bf16[384,4096]{1,0:T(8,128)(2,1)S(1)}, bf16[192,4096]{1,0:T(8,128)(2,1)S(1)}) custom-call(bf16[128,512]{1,0:T(8,128)(2,1)} %tok_hbm.1, bf16[128,512]{1,0:T(8,128)(2,1)} %og_hbm.1, s32[4,128]{1,0:T(4,128)} %bitcast.10, bf16[4,128]{1,0:T(4,128)(2,1)} %bitcast.11, bf16[384,4096]{1,0:T(8,128)(2,1)} %bitcast.6, ...), custom_call_target="tpu_custom_call" | custom-call | flops 12884901888 | bytes 16777216 | tf_op jit(solution)/shard_map/pallas_call | solution.py:526
  181.2 2.2 %shard_map.86 = (bf16[128,512]{1,0:T(8,128)(2,1)}, bf16[384,4096]{1,0:T(8,128)(2,1)}, bf16[192,4096]{1,0:T(8,128)(2,1)}) custom-call(bf16[128,512]{1,0:T(8,128)(2,1)S(1)} %get-tuple-element.9.in_grad, bf16[384,4096]{1,0:T(8,128)(2,1)S(1)} %get-tuple-element.10.grad_in, bf16[192,4096]{1,0:T(8,128)(2,1)S(1)} %get-tuple-element.11.grad_out), custom_call_target="tpu_custom_call" | custom-call | tf_op jit(solution)/shard_map/pallas_call | solution.py:594

commit v4 on v3

--- a/solution.py
+++ b/solution.py
@@ -44,6 +44,7 @@
     grad_in,
     grad_out,
     tok,
+    tok_far,
     og,
     xs,
     gs,
@@ -51,6 +52,7 @@
     wo,
     pack_x,
     pack_g,
+    pack_far,
     onehot,
     named,
     rank,
@@ -69,6 +71,8 @@
     full_rec,
     back,
     load_sem,
+    t_send,
+    t_recv,
     a_send,
     a_recv,
     ring_send,
@@ -132,7 +136,7 @@
         return c
 
     lax.fori_loop(1, n_ep, greet, 0)
-    for who in (sib, up, dn):
+    for who in (sib, up, dn, far):
         signal(e, who)
 
     load_tok, load_og, load_wi, load_wo = (
@@ -179,7 +183,10 @@
         scale = jnp.sum(hot * share[pl.ds(c, 1), :], axis=1, keepdims=True)
         return (dot(hot.astype(BF16), og[...], ROWS) * scale).astype(BF16)
 
-    def pack_rows(rows_of, pack, buf):
+    def rows_far(c):
+        return dot(onehot[block(c), :], tok_far[...], ROWS).astype(BF16)
+
+    def pack_rows(rows_of, pack, buf, slot):
         def one(r, c):
             j = peer(r)
             made = rows_of(j)
@@ -190,28 +197,26 @@
         lax.fori_loop(1, n_ep, one, 0)
         made = rows_of(e)
         for h in range(2):
-            buf[t * 2 + h, block(e), :] = made[:, h * uw : (h + 1) * uw]
-
-    packs, bufs = (pack_x, pack_g), (xs, gs)
+            buf[slot * 2 + h, block(e), :] = made[:, h * uw : (h + 1) * uw]
+
+    packs, bufs, own = (pack_x, pack_g, pack_far), (xs, gs, xs), (t, t, far)
 
     def rows_copy(which, h, j, at):
         return remote(
             packs[which].at[j, h],
-            bufs[which].at[t * 2 + h, block(at)],
+            bufs[which].at[own[which] * 2 + h, block(at)],
             a_send.at[which, h, j],
             a_recv.at[which, h, at],
             j,
             t,
         )
 
-    def dispatch(which):
-        for h in range(2):
-
-            def one(r, c, h=h):
-                rows_copy(which, h, peer(r), e).start()
-                return c
-
-            lax.fori_loop(1, n_ep, one, 0)
+    def dispatch(which, h):
+        def one(r, c):
+            rows_copy(which, h, peer(r), e).start()
+            return c
+
+        lax.fori_loop(1, n_ep, one, 0)
 
     def arrived(which, h):
         def one(r, c):
@@ -221,14 +226,18 @@
         lax.fori_loop(1, n_ep, one, 0)
 
     load_tok.wait()
-    pack_rows(rows_x, pack_x, xs)
+    pack_rows(rows_x, pack_x, xs, t)
     ab[...] = jnp.zeros_like(ab)
     dh[...] = jnp.zeros_like(dh)
-    pl.semaphore_wait(barrier, n_ep - 1 + 3)
-    dispatch(0)
+    pl.semaphore_wait(barrier, n_ep - 1 + 4)
+    tokens_far = remote(tok, tok_far, t_send.at[0], t_recv.at[0], e, far)
+    tokens_far.start()
+    dispatch(0, 0)
+    dispatch(0, 1)
     load_og.wait()
-    pack_rows(rows_g, pack_g, gs)
-    dispatch(1)
+    pack_rows(rows_g, pack_g, gs, t)
+    tokens_far.wait_recv()
+    pack_rows(rows_far, pack_far, xs, far)
     load_wi.wait()
     load_wo.wait()
 
@@ -248,50 +257,70 @@
     def got(which, slot, h):
         unit(which, slot, h, core_send.at[which, 0, h], sib).wait_recv()
 
-    def first_hop(which):
-        for h in range(2):
-            arrived(which, h)
-            to_up(which, h, t, h).start()
-            to_dn(which, h, t, h).start()
-            to_sib(which, 0, t, h).start()
-
-    def gather(which, use, between):
+    def first_hop(which, h):
+        arrived(which, h)
+        to_up(which, h, t, h).start()
+        to_dn(which, h, t, h).start()
+        to_sib(which, 0, t, h).start()
+
+    def gather_x(use):
         use(t, 0)
         use(t, 1)
         for h in range(2):
-            got(which, sib, h)
+            got(0, sib, h)
             use(sib, h)
-        got(which, dn, 0)
-        to_up(which, 2, dn, 0).start()
-        to_sib(which, 1, dn, 0).start()
-        got(which, up, 0)
-        to_sib(which, 2, up, 0).start()
+        for h in range(2):
+            got(0, dn, h)
+            to_sib(0, 1, dn, h).start()
+            got(0, up, h)
+            to_sib(0, 2, up, h).start()
+            if h == 1:
+                first_hop(1, 0)
+            use(dn, h)
+            use(up, h)
+            arrived(2, h)
+            to_sib(0, 3, far, h).start()
+            use(far, h)
+            for slot in (sdn, sup, sfar):
+                got(0, slot, h)
+                use(slot, h)
+
+    def gather_g(use):
+        use(t, 0)
+        use(t, 1)
+        for h in range(2):
+            got(1, sib, h)
+            use(sib, h)
+        got(1, dn, 0)
+        to_up(1, 2, dn, 0).start()
+        to_sib(1, 1, dn, 0).start()
+        got(1, up, 0)
+        to_sib(1, 2, up, 0).start()
         use(dn, 0)
         use(up, 0)
         for slot in (sdn, sup):
-            got(which, slot, 0)
+            got(1, slot, 0)
             use(slot, 0)
-        got(which, up, 1)
-        to_dn(which, 2, up, 1).start()
-        to_sib(which, 2, up, 1).start()
-        got(which, dn, 1)
-        to_sib(which, 1, dn, 1).start()
-        between()
+        got(1, up, 1)
+        to_dn(1, 2, up, 1).start()
+        to_sib(1, 2, up, 1).start()
+        got(1, dn, 1)
+        to_sib(1, 1, dn, 1).start()
         use(dn, 1)
         use(up, 1)
         for slot in (sdn, sup):
-            got(which, slot, 1)
+            got(1, slot, 1)
             use(slot, 1)
         for h in range(2):
-            got(which, far, h)
-            to_sib(which, 3, far, h).start()
+            got(1, far, h)
+            to_sib(1, 3, far, h).start()
             use(far, h)
         for h in range(2):
-            got(which, sfar, h)
+            got(1, sfar, h)
             use(sfar, h)
 
     def sent(which):
-        for n in range(3):
+        for n in range(2 + which):
             to_up(which, n, t, 0).wait_send()
             to_dn(which, n, t, 0).wait_send()
         for n in range(4):
@@ -336,8 +365,14 @@
 
         lax.fori_loop(0, rows // tile, one, 0)
 
-    first_hop(0)
-    gather(0, use_x, functools.partial(first_hop, 1))
+    first_hop(0, 0)
+    dispatch(2, 0)
+    dispatch(2, 1)
+    first_hop(0, 1)
+    dispatch(1, 0)
+    dispatch(1, 1)
+    gather_x(use_x)
+    first_hop(1, 1)
 
     def act(i, c):
         r = pl.ds(pl.multiple_of(i * lane, lane), lane)
@@ -346,7 +381,7 @@
         return c
 
     lax.fori_loop(0, rows // lane, act, 0)
-    gather(1, use_g, lambda: None)
+    gather_g(use_g)
 
     def act_grad(i, c):
         r = pl.ds(pl.multiple_of(i * lane, lane), lane)
@@ -478,7 +513,7 @@
 
     def end_peers(r, c):
         j = peer(r)
-        for which in range(2):
+        for which in range(3):
             for h in range(2):
                 rows_copy(which, h, j, e).wait_send()
         home(j, e).wait_send()
@@ -487,6 +522,7 @@
     lax.fori_loop(1, n_ep, end_peers, 0)
     sent(0)
     sent(1)
+    tokens_far.wait_send()
     far_dn.wait_send()
     far_up.wait_send()
     for direction in range(2):
@@ -535,10 +571,12 @@
         scratch_shapes=[
             pltpu.VMEM((ntok, width), BF16),
             pltpu.VMEM((ntok, width), BF16),
+            pltpu.VMEM((ntok, width), BF16),
             pltpu.VMEM((n_unit, rows, uw), BF16),
             pltpu.VMEM((n_unit, rows, uw), BF16),
             pltpu.VMEM((2 * ff, depth), BF16),
             pltpu.VMEM((ff, depth), BF16),
+            pltpu.VMEM((n_ep, 2, cap, uw), BF16),
             pltpu.VMEM((n_ep, 2, cap, uw), BF16),
             pltpu.VMEM((n_ep, 2, cap, uw), BF16),
             pltpu.VMEM((rows, ntok), BF16),
@@ -559,8 +597,10 @@
             pltpu.VMEM((2, rows, width), BF16),
             pltpu.VMEM((rows, width), BF16),
             dma((4,)),
-            dma((2, 2, n_ep)),
-            dma((2, 2, n_ep)),
+            dma((1,)),
+            dma((1,)),
+            dma((3, 2, n_ep)),
+            dma((3, 2, n_ep)),
             dma((2, 2, 3)),
             dma((2, 4, 2)),
             dma((2, n_unit)),

time: 186 us -> 176 us (0.946)
  Pallas kernels: 183 us -> 173 us
    pallas_call x1, Pallas kernels: 181 us -> 170 us  [body(): pl.pallas_call(functools.partial(kernel, n_ep, n_y), out_shape=(pltpu.VME...]
where the time goes in v4:
time: 176 us; the launch traced here: 173 us
  Pallas kernels  173 us (98%)
    pallas_call x1, Pallas kernels, body(): pl.pallas_call(functools.partial(kernel, n_ep, n_y), out_shape=(pltpu.VME...  170 us

profile of v4, /device:TPU:0, one launch (start us, length us, event | category | flops | bytes accessed | tf_op | source)
XLA Modules:
  0.0 173.3 jit_solution(11648023165229175425)
XLA Ops:
  0.6 170.4 %shard_map.85 = (bf16[128,512]{1,0:T(8,128)(2,1)S(1)}, bf16[384,4096]{1,0:T(8,128)(2,1)S(1)}, bf16[192,4096]{1,0:T(8,128)(2,1)S(1)}) custom-call(bf16[128,512]{1,0:T(8,128)(2,1)} %tok_hbm.1, bf16[128,512]{1,0:T(8,128)(2,1)} %og_hbm.1, s32[4,128]{1,0:T(4,128)} %bitcast.10, bf16[4,128]{1,0:T(4,128)(2,1)} %bitcast.11, bf16[384,4096]{1,0:T(8,128)(2,1)} %bitcast.6, ...), custom_call_target="tpu_custom_call" | custom-call | flops 12884901888 | bytes 16777216 | tf_op jit(solution)/shard_map/pallas_call | solution.py:562
  171.0 2.2 %shard_map.86 = (bf16[128,512]{1,0:T(8,128)(2,1)}, bf16[384,4096]{1,0:T(8,128)(2,1)}, bf16[192,4096]{1,0:T(8,128)(2,1)}) custom-call(bf16[128,512]{1,0:T(8,128)(2,1)S(1)} %get-tuple-element.9.in_grad, bf16[384,4096]{1,0:T(8,128)(2,1)S(1)} %get-tuple-element.10.grad_in, bf16[192,4096]{1,0:T(8,128)(2,1)S(1)} %get-tuple-element.11.grad_out), custom_call_target="tpu_custom_call" | custom-call | tf_op jit(solution)/shard_map/pallas_call | solution.py:634

commit v5 on v4

--- a/solution.py
+++ b/solution.py
@@ -1,4 +1,5 @@
 import functools
+import math
 
 import jax
 import jax.numpy as jnp
@@ -54,8 +55,7 @@
     pack_g,
     pack_far,
     onehot,
-    named,
-    rank,
+    codes,
     share,
     ab,
     dh,
@@ -70,6 +70,8 @@
     half_rec,
     full_rec,
     back,
+    token_sum,
+    token_rec,
     load_sem,
     t_send,
     t_recv,
@@ -78,6 +80,10 @@
     ring_send,
     core_send,
     g_recv,
+    fr_send,
+    fr_recv,
+    fc_send,
+    fc_recv,
     eo_send,
     eo_recv,
     ei_send,
@@ -88,12 +94,15 @@
     h_recv,
     f_send,
     f_recv,
-    b_send,
-    b_recv,
+    z_send,
+    z_recv,
+    c_send,
+    c_recv,
 ):
     n_unit, rows, uw = xs.shape
     cap = rows // n_ep
     half = rows // 2
+    uq = uw // 2
     width = tok.shape[1]
     ntok = tok.shape[0]
     ff = wo.shape[0]
@@ -109,6 +118,10 @@
     y_dn = lax.rem(y + n_y - 1, n_y)
     up, far, dn = (v * 2 + core for v in (y_up, y_far, y_dn))
     sup, sfar, sdn = (v * 2 + (1 - core) for v in (y_up, y_far, y_dn))
+    n_z = math.isqrt(n_ep)
+    n_x = n_ep // n_z
+    x = e // n_z
+    z = e % n_z
     other = lax.rem(e + n_ep // 2, n_ep)
 
     def remote(src, dst, send, recv, ep, tp):
@@ -161,43 +174,30 @@
         < lax.broadcasted_iota(jnp.int32, (ntok, ntok), 1)
     )
     before = jnp.where(before, 1.0, 0.0).astype(BF16)
-    named[...] = hits
-    rank[...] = dot(hits.astype(BF16), before, ROWS)
+    codes[x] = jnp.where(hits > 0.5, dot(hits.astype(BF16), before, ROWS), -1.0)
     share[...] = weights
     slots = lax.broadcasted_iota(jnp.int32, (cap, ntok), 0).astype(F32)
 
-    def place(c):
-        mine = (named[pl.ds(c, 1), :] > 0.5) & (rank[pl.ds(c, 1), :] == slots)
-        return jnp.where(mine, 1.0, 0.0)
+    def place(block_x, c):
+        return jnp.where(codes[block_x, pl.ds(c, 1), :] == slots, 1.0, 0.0)
 
     def block(c):
         return pl.ds(pl.multiple_of(c * cap, cap), cap)
 
-    def rows_x(c):
-        hot = place(c).astype(BF16)
-        onehot[block(c), :] = hot
-        return dot(hot, tok[...], ROWS).astype(BF16)
-
-    def rows_g(c):
-        hot = place(c)
-        scale = jnp.sum(hot * share[pl.ds(c, 1), :], axis=1, keepdims=True)
-        return (dot(hot.astype(BF16), og[...], ROWS) * scale).astype(BF16)
-
-    def rows_far(c):
-        return dot(onehot[block(c), :], tok_far[...], ROWS).astype(BF16)
-
-    def pack_rows(rows_of, pack, buf, slot):
-        def one(r, c):
-            j = peer(r)
-            made = rows_of(j)
-            for h in range(2):
-                pack[j, h] = made[:, h * uw : (h + 1) * uw]
-            return c
-
-        lax.fori_loop(1, n_ep, one, 0)
-        made = rows_of(e)
+    def pack_rows(source, pack, buf, slot, scaled):
+        group = min(4, n_ep)
+        for g in range(0, n_ep, group):
+            made = dot(onehot[g * cap : (g + group) * cap, :], source[...], ROWS)
+            for k in range(group):
+                c = g + k
+                rows_c = made[k * cap : (k + 1) * cap]
+                if scaled:
+                    hot = onehot[c * cap : (c + 1) * cap, :].astype(F32)
+                    rows_c = rows_c * jnp.sum(hot * share[c : c + 1, :], axis=1, keepdims=True)
+                for h in range(2):
+                    pack[c, h] = rows_c[:, h * uw : (h + 1) * uw].astype(BF16)
         for h in range(2):
-            buf[slot * 2 + h, block(e), :] = made[:, h * uw : (h + 1) * uw]
+            buf[slot * 2 + h, block(e), :] = pack[e, h]
 
     packs, bufs, own = (pack_x, pack_g, pack_far), (xs, gs, xs), (t, t, far)
 
@@ -225,21 +225,31 @@
 
         lax.fori_loop(1, n_ep, one, 0)
 
+    for c in range(n_ep):
+        onehot[c * cap : (c + 1) * cap, :] = place(x, c).astype(BF16)
     load_tok.wait()
-    pack_rows(rows_x, pack_x, xs, t)
-    ab[...] = jnp.zeros_like(ab)
-    dh[...] = jnp.zeros_like(dh)
+    pack_rows(tok, pack_x, xs, t, False)
     pl.semaphore_wait(barrier, n_ep - 1 + 4)
     tokens_far = remote(tok, tok_far, t_send.at[0], t_recv.at[0], e, far)
     tokens_far.start()
     dispatch(0, 0)
     dispatch(0, 1)
-    load_og.wait()
-    pack_rows(rows_g, pack_g, gs, t)
+
+    def code_copy(r, at):
+        to = lax.rem(x + r, n_x)
+        return remote(
+            codes.at[x], codes.at[at], c_send.at[0, r], c_recv.at[0, at], to * n_z + z, t
+        )
+
+    def send_code(r, c):
+        code_copy(r, x).start()
+        return c
+
+    lax.fori_loop(1, n_x, send_code, 0)
+    ab[...] = jnp.zeros_like(ab)
+    dh[...] = jnp.zeros_like(dh)
     tokens_far.wait_recv()
-    pack_rows(rows_far, pack_far, xs, far)
-    load_wi.wait()
-    load_wo.wait()
+    pack_rows(tok_far, pack_far, xs, far, False)
 
     def unit(which, slot, h, send, to):
         ref = bufs[which].at[slot * 2 + h]
@@ -285,14 +295,25 @@
                 got(0, slot, h)
                 use(slot, h)
 
-    def gather_g(use):
+    def quarter(slot, h, q, send, recv, to):
+        ref = gs.at[slot * 2 + h, :, q * uq : (q + 1) * uq]
+        return remote(ref, ref, send, recv, e, to)
+
+    def far_ring(slot, h, q):
+        return quarter(slot, h, q, fr_send.at[h, q], fr_recv.at[h, q], (up, dn)[h])
+
+    def far_core(slot, h, q):
+        return quarter(slot, h, q, fc_send.at[h, q], fc_recv.at[h, q], sib)
+
+    def gather_g(use, use_far):
         use(t, 0)
         use(t, 1)
         for h in range(2):
             got(1, sib, h)
             use(sib, h)
         got(1, dn, 0)
-        to_up(1, 2, dn, 0).start()
+        for q in range(2):
+            far_ring(dn, 0, q).start()
         to_sib(1, 1, dn, 0).start()
         got(1, up, 0)
         to_sib(1, 2, up, 0).start()
@@ -302,7 +323,8 @@
             got(1, slot, 0)
             use(slot, 0)
         got(1, up, 1)
-        to_dn(1, 2, up, 1).start()
+        for q in range(2):
+            far_ring(up, 1, q).start()
         to_sib(1, 2, up, 1).start()
         got(1, dn, 1)
         to_sib(1, 1, dn, 1).start()
@@ -311,19 +333,20 @@
         for slot in (sdn, sup):
             got(1, slot, 1)
             use(slot, 1)
-        for h in range(2):
-            got(1, far, h)
-            to_sib(1, 3, far, h).start()
-            use(far, h)
-        for h in range(2):
-            got(1, sfar, h)
-            use(sfar, h)
+        for q in range(2):
+            for h in range(2):
+                far_ring(far, h, q).wait_recv()
+                far_core(far, h, q).start()
+                use_far(far, h, q)
+            for h in range(2):
+                far_core(sfar, h, q).wait_recv()
+                use_far(sfar, h, q)
 
     def sent(which):
-        for n in range(2 + which):
+        for n in range(2):
             to_up(which, n, t, 0).wait_send()
             to_dn(which, n, t, 0).wait_send()
-        for n in range(4):
+        for n in range(4 - which):
             for h in range(2):
                 to_sib(which, n, t, h).wait_send()
 
@@ -343,9 +366,15 @@
 
         lax.fori_loop(0, rows // tile, one, 0)
 
-    def send_out(u):
+    def send_out(u, q):
+        w = pl.ds(pl.multiple_of(u * uw + q * uq, uq), uq)
         return remote(
-            own_out.at[u], grad_out.at[:, ucolumns(u)], eo_send.at[u], eo_recv.at[u], other, t
+            own_out.at[u, :, q * uq : (q + 1) * uq],
+            grad_out.at[:, w],
+            eo_send.at[u, q],
+            eo_recv.at[u, q],
+            other,
+            t,
         )
 
     def send_in(u):
@@ -356,7 +385,8 @@
     def use_g(slot, h):
         u = slot * 2 + h
         own_out[u] = dot(hid[...], gs[u], ROWS).astype(BF16)
-        send_out(u).start()
+        for q in range(2):
+            send_out(u, q).start()
 
         def one(i, c):
             r = pl.ds(pl.multiple_of(i * tile, tile), tile)
@@ -365,10 +395,28 @@
 
         lax.fori_loop(0, rows // tile, one, 0)
 
+    def use_g_far(slot, h, q):
+        u = slot * 2 + h
+        w = slice(q * uq, (q + 1) * uq)
+        own_out[u, :, w] = dot(hid[...], gs[u, :, w], ROWS).astype(BF16)
+        send_out(u, q).start()
+        cols = pl.ds(pl.multiple_of(u * uw + q * uq, uq), uq)
+
+        def one(i, c):
+            r = pl.ds(pl.multiple_of(i * tile, tile), tile)
+            dh[:, r] += dot(wo[:, cols], gs[u, r, w], LAST)
+            return c
+
+        lax.fori_loop(0, rows // tile, one, 0)
+
     first_hop(0, 0)
     dispatch(2, 0)
     dispatch(2, 1)
     first_hop(0, 1)
+    load_og.wait()
+    pack_rows(og, pack_g, gs, t, True)
+    load_wi.wait()
+    load_wo.wait()
     dispatch(1, 0)
     dispatch(1, 1)
     gather_x(use_x)
@@ -381,7 +429,7 @@
         return c
 
     lax.fori_loop(0, rows // lane, act, 0)
-    gather_g(use_g)
+    gather_g(use_g, use_g_far)
 
     def act_grad(i, c):
         r = pl.ds(pl.multiple_of(i * lane, lane), lane)
@@ -478,30 +526,76 @@
 
     lax.fori_loop(0, n_ep, total, 0)
 
-    def home(j, at):
-        return remote(part.at[y, block(j)], back.at[block(at)], b_send.at[j], b_recv.at[at], j, t)
-
-    def send_home(r, c):
-        home(peer(r), e).start()
-        return c
-
-    lax.fori_loop(1, n_ep, send_home, 0)
-    back[block(e), :] = part[y, block(e), :]
+    def along_z(r, at, bx):
+        to = lax.rem(z + r, n_z)
+        return remote(
+            part.at[y, block(bx * n_z + to)],
+            back.at[bx, at],
+            z_send.at[r, bx],
+            z_recv.at[at, bx],
+            x * n_z + to,
+            t,
+        )
+
+    def send_z(r, c):
+        for bx in range(n_x):
+            along_z(r, z, bx).start()
+        return c
+
+    lax.fori_loop(1, n_z, send_z, 0)
+    for bx in range(n_x):
+        back[bx, z] = part[y, block(bx * n_z + z), :]
 
     def merge_out(u, c):
-        send_out(u).wait_recv()
+        for q in range(2):
+            send_out(u, q).wait_recv()
         w = ucolumns(u)
         grad_out[:, w] = (grad_out[:, w].astype(F32) + own_out[u].astype(F32)).astype(BF16)
         return c
 
     lax.fori_loop(0, n_unit, merge_out, 0)
 
-    def got_home(r, c):
-        home(peer(r), peer(r)).wait_recv()
-        return c
-
-    lax.fori_loop(1, n_ep, got_home, 0)
-    in_grad[...] = dot(onehot[...], back[...], FIRST).astype(BF16)
+    def got_code(r, c):
+        code_copy(r, lax.rem(x + r, n_x)).wait_recv()
+        return c
+
+    lax.fori_loop(1, n_x, got_code, 0)
+
+    def got_z(r, c):
+        for bx in range(n_x):
+            along_z(r, lax.rem(z + r, n_z), bx).wait_recv()
+        return c
+
+    lax.fori_loop(1, n_z, got_z, 0)
+
+    def along_x(r, at):
+        to = lax.rem(x + r, n_x)
+        return remote(
+            token_sum.at[to], token_rec.at[at], c_send.at[1, r], c_recv.at[1, at], to * n_z + z, t
+        )
+
+    def by_token(r, c):
+        bx = lax.rem(x + r, n_x)
+        hot = jnp.concatenate([place(bx, x * n_z + k) for k in range(n_z)], axis=0).astype(BF16)
+        returned = jnp.concatenate([back[bx, k] for k in range(n_z)], axis=0)
+        token_sum[bx] = dot(hot, returned, FIRST).astype(BF16)
+        return c
+
+    def send_x(r, c):
+        by_token(r, c)
+        along_x(r, x).start()
+        return c
+
+    lax.fori_loop(1, n_x, send_x, 0)
+    by_token(0, 0)
+    token_rec[x] = token_sum[x]
+
+    def got_x(r, c):
+        along_x(r, lax.rem(x + r, n_x)).wait_recv()
+        return c
+
+    lax.fori_loop(1, n_x, got_x, 0)
+    in_grad[...] = jnp.sum(token_rec[...].astype(F32), axis=0).astype(BF16)
 
     def merge_in(u, c):
         send_in(u).wait_recv()
@@ -516,13 +610,30 @@
         for which in range(3):
             for h in range(2):
                 rows_copy(which, h, j, e).wait_send()
-        home(j, e).wait_send()
         return c
 
     lax.fori_loop(1, n_ep, end_peers, 0)
+
+    def end_z(r, c):
+        for bx in range(n_x):
+            along_z(r, z, bx).wait_send()
+        return c
+
+    lax.fori_loop(1, n_z, end_z, 0)
+
+    def end_x(r, c):
+        code_copy(r, x).wait_send()
+        along_x(r, x).wait_send()
+        return c
+
+    lax.fori_loop(1, n_x, end_x, 0)
     sent(0)
     sent(1)
     tokens_far.wait_send()
+    for h in range(2):
+        for q in range(2):
+            far_ring(far, h, q).wait_send()
+            far_core(far, h, q).wait_send()
     far_dn.wait_send()
     far_up.wait_send()
     for direction in range(2):
@@ -536,7 +647,8 @@
     lax.fori_loop(0, n_y, end_parts, 0)
 
     def end_grads(u, c):
-        send_out(u).wait_send()
+        for q in range(2):
+            send_out(u, q).wait_send()
         send_in(u).wait_send()
         return c
 
@@ -548,6 +660,8 @@
     n_tp = lax.axis_size("tp")
     n_y = n_tp // 2
     n_unit = 2 * n_tp
+    n_z = math.isqrt(n_ep)
+    n_x = n_ep // n_z
     ntok, top = routes.shape
     cap = 2 * ntok * top // n_ep
     rows = n_ep * cap
@@ -580,8 +694,7 @@
             pltpu.VMEM((n_ep, 2, cap, uw), BF16),
             pltpu.VMEM((n_ep, 2, cap, uw), BF16),
             pltpu.VMEM((rows, ntok), BF16),
-            pltpu.VMEM((n_ep, ntok), F32),
-            pltpu.VMEM((n_ep, ntok), F32),
+            pltpu.VMEM((n_x, n_ep, ntok), F32),
             pltpu.VMEM((n_ep, ntok), F32),
             pltpu.VMEM((2 * ff, rows), F32),
             pltpu.VMEM((ff, rows), F32),
@@ -595,17 +708,23 @@
             pltpu.VMEM((n_y, rows, width), BF16),
             pltpu.VMEM((1, rows, width), BF16),
             pltpu.VMEM((2, rows, width), BF16),
-            pltpu.VMEM((rows, width), BF16),
+            pltpu.VMEM((n_x, n_z, cap, width), BF16),
+            pltpu.VMEM((n_x, ntok, width), BF16),
+            pltpu.VMEM((n_x, ntok, width), BF16),
             dma((4,)),
             dma((1,)),
             dma((1,)),
             dma((3, 2, n_ep)),
             dma((3, 2, n_ep)),
-            dma((2, 2, 3)),
+            dma((2, 2, 2)),
             dma((2, 4, 2)),
             dma((2, n_unit)),
-            dma((n_unit,)),
-            dma((n_unit,)),
+            dma((2, 2)),
+            dma((2, 2)),
+            dma((2, 2)),
+            dma((2, 2)),
+            dma((n_unit, 2)),
+            dma((n_unit, 2)),
             dma((n_unit,)),
             dma((n_unit,)),
             dma((n_y,)),
@@ -614,8 +733,10 @@
             dma((2,)),
             dma((2, 2)),
             dma((2, 2)),
-            dma((n_ep,)),
-            dma((n_ep,)),
+            dma((n_z, n_x)),
+            dma((n_z, n_x)),
+            dma((2, n_x)),
+            dma((2, n_x)),
         ],
         compiler_params=pltpu.CompilerParams(
             collective_id=0, has_side_effects=True, vmem_limit_bytes=56 * 1024 * 1024

time: 176 us -> 170 us (0.966); the launches traced: 173 us -> 170 us
  Pallas kernels: 173 us -> 169 us
    pallas_call x1, Pallas kernels: 170 us -> 167 us  [body(): pl.pallas_call(functools.partial(kernel, n_ep, n_y), out_shape=(pltpu.VME...]
where the time goes in v5:
time: 170 us
  Pallas kernels  169 us (99%)
    pallas_call x1, Pallas kernels, body(): pl.pallas_call(functools.partial(kernel, n_ep, n_y), out_shape=(pltpu.VME...  167 us

profile of v5, /device:TPU:0, one launch (start us, length us, event | category | flops | bytes accessed | tf_op | source)
XLA Modules:
  0.0 169.6 jit_solution(8227616710914929936)
XLA Ops:
  0.6 166.5 %shard_map.85 = (bf16[128,512]{1,0:T(8,128)(2,1)S(1)}, bf16[384,4096]{1,0:T(8,128)(2,1)S(1)}, bf16[192,4096]{1,0:T(8,128)(2,1)S(1)}) custom-call(bf16[128,512]{1,0:T(8,128)(2,1)} %tok_hbm.1, bf16[128,512]{1,0:T(8,128)(2,1)} %og_hbm.1, s32[4,128]{1,0:T(4,128)} %bitcast.10, bf16[4,128]{1,0:T(4,128)(2,1)} %bitcast.11, bf16[384,4096]{1,0:T(8,128)(2,1)} %bitcast.6, ...), custom_call_target="tpu_custom_call" | custom-call | flops 12884901888 | bytes 16777216 | tf_op jit(solution)/shard_map/pallas_call | solution.py:676
  167.2 2.2 %shard_map.86 = (bf16[128,512]{1,0:T(8,128)(2,1)}, bf16[384,4096]{1,0:T(8,128)(2,1)}, bf16[192,4096]{1,0:T(8,128)(2,1)}) custom-call(bf16[128,512]{1,0:T(8,128)(2,1)S(1)} %get-tuple-element.9.in_grad, bf16[384,4096]{1,0:T(8,128)(2,1)S(1)} %get-tuple-element.10.grad_in, bf16[192,4096]{1,0:T(8,128)(2,1)S(1)} %get-tuple-element.11.grad_out), custom_call_target="tpu_custom_call" | custom-call | tf_op jit(solution)/shard_map/pallas_call | solution.py:755

commit v6 on v5

--- a/solution.py
+++ b/solution.py
@@ -184,18 +184,19 @@
     def block(c):
         return pl.ds(pl.multiple_of(c * cap, cap), cap)
 
+    def weighted(c):
+        return jnp.where(codes[x, pl.ds(c, 1), :] == slots, share[pl.ds(c, 1), :], 0.0)
+
     def pack_rows(source, pack, buf, slot, scaled):
         group = min(4, n_ep)
         for g in range(0, n_ep, group):
-            made = dot(onehot[g * cap : (g + group) * cap, :], source[...], ROWS)
+            hot = onehot[g * cap : (g + group) * cap, :]
+            if scaled:
+                hot = jnp.concatenate([weighted(g + k) for k in range(group)]).astype(BF16)
+            made = dot(hot, source[...], ROWS).astype(BF16)
             for k in range(group):
-                c = g + k
-                rows_c = made[k * cap : (k + 1) * cap]
-                if scaled:
-                    hot = onehot[c * cap : (c + 1) * cap, :].astype(F32)
-                    rows_c = rows_c * jnp.sum(hot * share[c : c + 1, :], axis=1, keepdims=True)
                 for h in range(2):
-                    pack[c, h] = rows_c[:, h * uw : (h + 1) * uw].astype(BF16)
+                    pack[g + k, h] = made[k * cap : (k + 1) * cap, h * uw : (h + 1) * uw]
         for h in range(2):
             buf[slot * 2 + h, block(e), :] = pack[e, h]
 
@@ -280,12 +281,14 @@
             got(0, sib, h)
             use(sib, h)
         for h in range(2):
+            if h == 1:
+                first_hop(1, 0)
             got(0, dn, h)
             to_sib(0, 1, dn, h).start()
             got(0, up, h)
             to_sib(0, 2, up, h).start()
             if h == 1:
-                first_hop(1, 0)
+                first_hop(1, 1)
             use(dn, h)
             use(up, h)
             arrived(2, h)
@@ -420,7 +423,6 @@
     dispatch(1, 0)
     dispatch(1, 1)
     gather_x(use_x)
-    first_hop(1, 1)
 
     def act(i, c):
         r = pl.ds(pl.multiple_of(i * lane, lane), lane)
@@ -458,16 +460,6 @@
 
     def send_part(at):
         return remote(part_sib.at[at], part_rec.at[at], p_send.at[at], p_recv.at[at], e, sib)
-
-    for i, (yd, slot) in enumerate(((y_far, sfar), (y_up, sup), (y_dn, sdn), (y, sib))):
-        wgrad_in(2 * i)
-        wgrad_in(2 * i + 1)
-        term(slot, part_sib, yd)
-        send_part(yd).start()
-    for i, (yd, slot) in enumerate(((y_far, far), (y_up, up), (y_dn, dn), (y, t))):
-        wgrad_in(8 + 2 * i)
-        wgrad_in(9 + 2 * i)
-        term(slot, part, yd)
 
     def add(ref, at, src, src_at, h):
         r = pl.ds(h * half, half)
@@ -498,19 +490,43 @@
             to,
         )
 
+    def term_sib(slot, at):
+        term(slot, part_sib, at)
+        send_part(at).start()
+
+    wgrad_in(0)
+    wgrad_in(1)
+    term_sib(sfar, y_far)
+    term(far, part, y_far)
+    term_sib(sdn, y_dn)
+    term_sib(sup, y_up)
     chip(y_far)
     far_dn.start()
     far_up.start()
+    wgrad_in(2)
+    wgrad_in(3)
+    term(dn, part, y_dn)
+    term(up, part, y_up)
     chip(y_dn)
     full(0, 1).start()
     chip(y_up)
     full(1, 0).start()
+    wgrad_in(4)
+    wgrad_in(5)
+    term_sib(sib, y)
+    wgrad_in(6)
+    wgrad_in(7)
+    term(t, part, y)
+    for u in range(8, 12):
+        wgrad_in(u)
     far_dn.wait_recv()
     add(part, y_dn, half_rec, 0, 0)
     full(0, 0).start()
     far_up.wait_recv()
     add(part, y_up, half_rec, 0, 1)
     full(1, 1).start()
+    for u in range(12, 16):
+        wgrad_in(u)
     send_part(y).wait_recv()
 
     for h in range(2):
@@ -596,14 +612,6 @@
 
     lax.fori_loop(1, n_x, got_x, 0)
     in_grad[...] = jnp.sum(token_rec[...].astype(F32), axis=0).astype(BF16)
-
-    def merge_in(u, c):
-        send_in(u).wait_recv()
-        w = ucolumns(u)
-        grad_in[:, w] = (grad_in[:, w].astype(F32) + own_in[u].astype(F32)).astype(BF16)
-        return c
-
-    lax.fori_loop(0, n_unit, merge_in, 0)
 
     def end_peers(r, c):
         j = peer(r)
@@ -649,10 +657,18 @@
     def end_grads(u, c):
         for q in range(2):
             send_out(u, q).wait_send()
+        return c
+
+    lax.fori_loop(0, n_unit, end_grads, 0)
+
+    def merge_in(u, c):
+        send_in(u).wait_recv()
+        w = ucolumns(u)
+        grad_in[:, w] = (grad_in[:, w].astype(F32) + own_in[u].astype(F32)).astype(BF16)
         send_in(u).wait_send()
         return c
 
-    lax.fori_loop(0, n_unit, end_grads, 0)
+    lax.fori_loop(0, n_unit, merge_in, 0)
 
 
 def body(tokens, out_grad, routes, probs, w_in, w_out):

time: 170 us -> 168 us (0.988)
  Pallas kernels: 169 us -> 167 us
    pallas_call x1, Pallas kernels: 167 us -> 165 us  [body(): pl.pallas_call(functools.partial(kernel, n_ep, n_y), out_shape=(pltpu.VME...]
where the time goes in v6:
time: 168 us
  Pallas kernels  167 us (99%)
    pallas_call x1, Pallas kernels, body(): pl.pallas_call(functools.partial(kernel, n_ep, n_y), out_shape=(pltpu.VME...  165 us

profile of v6, /device:TPU:0, one launch (start us, length us, event | category | flops | bytes accessed | tf_op | source)
XLA Modules:
  0.0 167.6 jit_solution(6518665194265632139)
XLA Ops:
  0.6 164.5 %shard_map.85 = (bf16[128,512]{1,0:T(8,128)(2,1)S(1)}, bf16[384,4096]{1,0:T(8,128)(2,1)S(1)}, bf16[192,4096]{1,0:T(8,128)(2,1)S(1)}) custom-call(bf16[128,512]{1,0:T(8,128)(2,1)} %tok_hbm.1, bf16[128,512]{1,0:T(8,128)(2,1)} %og_hbm.1, s32[4,128]{1,0:T(4,128)} %bitcast.10, bf16[4,128]{1,0:T(4,128)(2,1)} %bitcast.11, bf16[384,4096]{1,0:T(8,128)(2,1)} %bitcast.6, ...), custom_call_target="tpu_custom_call" | custom-call | flops 12884901888 | bytes 16777216 | tf_op jit(solution)/shard_map/pallas_call | solution.py:692
  165.2 2.2 %shard_map.86 = (bf16[128,512]{1,0:T(8,128)(2,1)}, bf16[384,4096]{1,0:T(8,128)(2,1)}, bf16[192,4096]{1,0:T(8,128)(2,1)}) custom-call(bf16[128,512]{1,0:T(8,128)(2,1)S(1)} %get-tuple-element.9.in_grad, bf16[384,4096]{1,0:T(8,128)(2,1)S(1)} %get-tuple-element.10.grad_in, bf16[192,4096]{1,0:T(8,128)(2,1)S(1)} %get-tuple-element.11.grad_out), custom_call_target="tpu_custom_call" | custom-call | tf_op jit(solution)/shard_map/pallas_call | solution.py:771

commit v7 on v6

--- a/solution.py
+++ b/solution.py
@@ -285,10 +285,10 @@
                 first_hop(1, 0)
             got(0, dn, h)
             to_sib(0, 1, dn, h).start()
+            if h == 1:
+                first_hop(1, 1)
             got(0, up, h)
             to_sib(0, 2, up, h).start()
-            if h == 1:
-                first_hop(1, 1)
             use(dn, h)
             use(up, h)
             arrived(2, h)

time: 168 us -> 168 us (level)
  no operation moved by 1% of the time
where the time goes in v7:
time: 168 us
  Pallas kernels  167 us (99%)
    pallas_call x1, Pallas kernels, body(): pl.pallas_call(functools.partial(kernel, n_ep, n_y), out_shape=(pltpu.VME...  165 us

profile of v7, /device:TPU:0, one launch (start us, length us, event | category | flops | bytes accessed | tf_op | source)
XLA Modules:
  0.0 167.6 jit_solution(2619013772049125559)
XLA Ops:
  0.6 164.5 %shard_map.85 = (bf16[128,512]{1,0:T(8,128)(2,1)S(1)}, bf16[384,4096]{1,0:T(8,128)(2,1)S(1)}, bf16[192,4096]{1,0:T(8,128)(2,1)S(1)}) custom-call(bf16[128,512]{1,0:T(8,128)(2,1)} %tok_hbm.1, bf16[128,512]{1,0:T(8,128)(2,1)} %og_hbm.1, s32[4,128]{1,0:T(4,128)} %bitcast.10, bf16[4,128]{1,0:T(4,128)(2,1)} %bitcast.11, bf16[384,4096]{1,0:T(8,128)(2,1)} %bitcast.6, ...), custom_call_target="tpu_custom_call" | custom-call | flops 12884901888 | bytes 16777216 | tf_op jit(solution)/shard_map/pallas_call | solution.py:692
  165.2 2.2 %shard_map.86 = (bf16[128,512]{1,0:T(8,128)(2,1)}, bf16[384,4096]{1,0:T(8,128)(2,1)}, bf16[192,4096]{1,0:T(8,128)(2,1)}) custom-call(bf16[128,512]{1,0:T(8,128)(2,1)S(1)} %get-tuple-element.9.in_grad, bf16[384,4096]{1,0:T(8,128)(2,1)S(1)} %get-tuple-element.10.grad_in, bf16[192,4096]{1,0:T(8,128)(2,1)S(1)} %get-tuple-element.11.grad_out), custom_call_target="tpu_custom_call" | custom-call | tf_op jit(solution)/shard_map/pallas_call | solution.py:771
